TPU v7x, 128 devices: a whole 4x4x4 slice. The times are simulated.
128 devices in a mesh: dp: 4 (over x_hi, core), space: 32 (over x_lo, y, z).
Axes of the slice: x: 4 (x_hi: 2, x_lo: 2; x = x_hi * 2 + x_lo), y: 4, z: 4, core: 2. Of those that a mesh axis runs over, the one named last changes fastest.
Arguments:
- samples: bfloat16 [4, 320, 720, 512], P('dp', 'space'), may hold values from -6 to 6
- norm_gain: float32 [512], replicated, may hold values from 0.1 to 1.9
- norm_bias: float32 [512], replicated, may hold values from -3 to 3
- spectral_filter: float32 [320, 512, 722], P(None, ('dp', 'space')), may hold values from -4.5 to 4.5
Outputs:
- updated: bfloat16 [4, 320, 720, 512], P('dp', 'space')
All inputs are finite; a program needn't handle non-finite values.
Results may differ from a plain program's by a relative error of at most 0.015.
Values may be sent and summed in bfloat16 or wider, within the bound.
No kernel may reach another device: no remote copies, remote signals or barrier semaphores. Data moves between devices by JAX's collectives and lax.ppermute only.
A program may use at most 192 MiB of HBM per device.

v0:
```python
import math

import jax
import jax.numpy as jnp
from jax import lax
from jax.sharding import PartitionSpec as P


def dft_tables(lat_len, lon_len):
    freqs = lon_len // 2 + 1
    lon_index = jnp.arange(lon_len, dtype=jnp.int32)
    freq_index = jnp.arange(freqs, dtype=jnp.int32)
    turns = (lon_index[:, None] * freq_index[None, :] % lon_len).astype(jnp.float32) * (
        2.0 * math.pi / lon_len
    )
    lon_scale = 1.0 / math.sqrt(lon_len)
    row_forward = (jnp.concatenate([jnp.cos(turns), -jnp.sin(turns)], axis=1) * lon_scale).astype(
        jnp.bfloat16
    )
    weights = jnp.where((freq_index == 0) | (freq_index == lon_len // 2), 1.0, 2.0).astype(
        jnp.float32
    )
    row_inverse = (
        jnp.concatenate(
            [weights[:, None] * jnp.cos(turns).T, -weights[:, None] * jnp.sin(turns).T], axis=0
        )
        * lon_scale
    ).astype(jnp.bfloat16)
    lat_index = jnp.arange(lat_len, dtype=jnp.int32)
    lat_turns = (lat_index[:, None] * lat_index[None, :] % lat_len).astype(jnp.float32) * (
        2.0 * math.pi / lat_len
    )
    lat_scale = 1.0 / math.sqrt(lat_len)
    col_cosine = (jnp.cos(lat_turns) * lat_scale).astype(jnp.bfloat16)
    col_sine = (jnp.sin(lat_turns) * lat_scale).astype(jnp.bfloat16)
    return (row_forward, row_inverse, col_cosine, col_sine)


def layer_norm(values, norm_gain, norm_bias):
    wide = values.astype(jnp.float32)
    center = jnp.mean(wide, axis=-1, keepdims=True)
    spread = jnp.mean(jnp.square(wide - center), axis=-1, keepdims=True)
    return ((wide - center) * lax.rsqrt(spread + 1e-05) * norm_gain + norm_bias).astype(
        jnp.bfloat16
    )


def column_forward(slab, col_cosine, col_sine):
    half_len = slab.shape[-1] // 2
    first = jnp.einsum("gh,shck->sgck", col_cosine, slab, preferred_element_type=jnp.float32)
    second = jnp.einsum("gh,shck->sgck", col_sine, slab, preferred_element_type=jnp.float32)
    return (
        first[..., :half_len] + second[..., half_len:],
        first[..., half_len:] - second[..., :half_len],
    )


def filter_inverse(spec_re, spec_im, filt_part, col_cosine, col_sine):
    half_len = spec_re.shape[-1]
    filt_re = filt_part[..., :half_len]
    filt_im = filt_part[..., half_len:]
    mixed = jnp.concatenate(
        [spec_re * filt_re - spec_im * filt_im, spec_re * filt_im + spec_im * filt_re], axis=-1
    ).astype(jnp.bfloat16)
    first = jnp.einsum("gh,shck->sgck", col_cosine, mixed, preferred_element_type=jnp.float32)
    second = jnp.einsum("gh,shck->sgck", col_sine, mixed, preferred_element_type=jnp.float32)
    return jnp.concatenate(
        [
            first[..., :half_len] - second[..., half_len:],
            first[..., half_len:] + second[..., :half_len],
        ],
        axis=-1,
    ).astype(jnp.bfloat16)


def shards(samples, norm_gain, norm_bias, spectral_filter):
    grid = samples[0]
    row_count, lon_len, channels = grid.shape
    dp_count = lax.axis_size("dp")
    space_count = lax.axis_size("space")
    lat_len = row_count * space_count
    chan_part = channels // (dp_count * space_count)
    row_forward, row_inverse, col_cosine, col_sine = dft_tables(lat_len, lon_len)
    normed = layer_norm(grid, norm_gain, norm_bias)
    rowspec = jnp.einsum(
        "rwc,wk->rck", normed, row_forward, preferred_element_type=jnp.float32
    ).astype(jnp.bfloat16)
    spec_len = rowspec.shape[-1]
    pieces = rowspec.reshape(row_count, dp_count, space_count, chan_part, spec_len)
    slab = lax.all_to_all(pieces, "space", split_axis=2, concat_axis=0, tiled=True).reshape(
        1, lat_len, dp_count * chan_part, spec_len
    )
    spec_re, spec_im = column_forward(slab, col_cosine, col_sine)
    back = filter_inverse(
        spec_re,
        spec_im,
        lax.all_gather(spectral_filter.astype(jnp.bfloat16), "dp", axis=1, tiled=True).astype(
            jnp.float32
        ),
        col_cosine,
        col_sine,
    )
    back = back.reshape(lat_len, dp_count, 1, chan_part, spec_len)
    returned = lax.all_to_all(back, "space", split_axis=0, concat_axis=2, tiled=True).reshape(
        row_count, channels, spec_len
    )
    branch = jnp.einsum("rck,kw->rwc", returned, row_inverse, preferred_element_type=jnp.float32)
    return (grid.astype(jnp.float32) + branch).astype(jnp.bfloat16)[None]


def solution(mesh):
    placed = (P("dp", "space", None, None), P(), P(), P(None, ("dp", "space"), None))
    return jax.shard_map(
        shards, mesh=mesh, in_specs=placed, out_specs=P("dp", "space", None, None), check_vma=False
    )
```

profile of v0, /device:TPU:14, one launch (start us, length us, event | category | flops | bytes accessed | tf_op | source)
XLA Modules:
  0.0 456.9 jit_solution(12482940291377291380)
XLA Ops:
  6.5 4.1 copy.32
  10.7 4.6 %sine_negate_fusion = (f32[720,361]{1,0:T(8,128)S(1)}, f32[720,361]{1,0:T(8,128)S(1)}) fusion(), kind=kLoop, calls=%fused_computation.52 | loop fusion | flops 2599200 | bytes 2079360 | tf_op jit(solution)/shard_map/neg | solution.py:17
  15.3 4.2 convert_reduce_fusion
  19.6 3.4 fusion.4
  23.1 11.9 %fusion.19 = bf16[10,512,722]{1,2,0:T(8,128)(2,1)} fusion(bf16[1,10,720,512]{3,2,1,0:T(8,128)(2,1)S(1)} %bitcast.100, f32[512]{0:T(512)S(1)} %copy-done.1, f32[512]{0:T(512)S(1)} %copy-done.2, f32[10,720]{1,0:T(8,128)S(1)} %add_rsqrt_fusion, f32[10,720]{1,0:T(8,128)S(1)} %broadcast_multiply_fusion, f32[720,361]{1,0:T(8,128)S(1)} %get-tuple-element.9, ...), kind=kOutput, calls=%fused_computation.34 | convolution fusion | flops 5350536192 | bytes 16907136 | tf_op jit(solution)/shard_map/rwc,wk->rck/dot_general | solution.py:85
  34.9 10.5 %copy.17 = bf16[10,512,722]{2,1,0:T(8,128)(2,1)} copy(bf16[10,512,722]{1,2,0:T(8,128)(2,1)} %fusion.19) | data formatting | bytes 14786560 | tf_op jit(solution)/shard_map/convert_element_type | solution.py:87
  45.4 14.0 %reshape.104 = bf16[10,4,32,4,722]{4,3,2,1,0:T(4,128)(2,1)} reshape(bf16[10,512,722]{2,1,0:T(8,128)(2,1)} %copy.17) | data formatting | bytes 14786560 | tf_op jit(solution)/shard_map/reshape | solution.py:89
  59.4 10.4 %copy.18 = bf16[10,4,32,4,722]{4,3,1,0,2:T(4,128)(2,1)} copy(bf16[10,4,32,4,722]{4,3,2,1,0:T(4,128)(2,1)} %reshape.104) | data formatting | bytes 14786560 | tf_op jit(solution)/shard_map/reshape | solution.py:89
  69.8 98.7 %all_to_all.30 = bf16[10,4,32,4,722]{4,3,1,0,2:T(4,128)(2,1)} all-to-all(bf16[10,4,32,4,722]{4,3,1,0,2:T(4,128)(2,1)} %copy.18), channel_id=1, replica_groups=mesh['dp'=4,'space'=32] {'space'}, dimensions={2} | all-to-all | bytes 14786560 | tf_op jit(solution)/shard_map/all_to_all | solution.py:90
  168.5 13.3 %reshape.105 = bf16[320,16,722]{2,1,0:T(8,128)(2,1)} reshape(bf16[32,10,4,1,4,722]{5,4,2,1,0,3:T(4,128)(2,1)} %bitcast.98) | data formatting | bytes 14786560 | tf_op jit(solution)/shard_map/reshape.1
  181.9 15.1 %convolution_bitcast_fusion.2 = f32[1,320,16,722]{3,1,2,0:T(8,128)} fusion(bf16[320,16,722]{2,1,0:T(8,128)(2,1)} %reshape.105), kind=kOutput, calls=%fused_computation.13 | convolution fusion | flops 2366976000 | bytes 22179840 | tf_op jit(solution)/shard_map/gh,shck->sgck/dot_general | solution.py:51
  196.9 11.7 %convolution_bitcast_fusion.3 = f32[1,320,16,722]{3,1,2,0:T(8,128)} fusion(bf16[320,16,722]{2,1,0:T(8,128)(2,1)S(1)} %copy-done), kind=kOutput, calls=%fused_computation.14 | convolution fusion | flops 2366976000 | bytes 22179840 | tf_op jit(solution)/shard_map/gh,shck->sgck/dot_general | solution.py:50
  208.7 10.4 %convert_element_type.85 = f32[320,16,722]{2,0,1:T(8,128)} convert(bf16[320,16,722]{2,0,1:T(8,128)(2,1)} %all-gather.2.cloned.1.call-done) | non-fusion elementwise | flops 3696640 | bytes 22179840 | tf_op jit(solution)/shard_map/convert_element_type | solution.py:97
  219.1 18.9 %fusion.23 = (bf16[320,16,361]{2,0,1:T(8,128)(2,1)S(1)}, bf16[320,16,361]{2,0,1:T(8,128)(2,1)S(1)}) fusion(f32[320,16,722]{2,0,1:T(8,128)} %convert_element_type.85, f32[1,320,16,722]{3,1,2,0:T(8,128)} %convolution_bitcast_fusion.2, f32[1,320,16,722]{3,1,2,0:T(8,128)} %convolution_bitcast_fusion.3), kind=kLoop, calls=%fused_computation.36 | loop fusion | flops 18483200 | bytes 51752960 | tf_op jit(solution)/shard_map/concatenate | solution.py:62
  238.1 12.2 %convolution_bitcast_fusion.1 = f32[1,320,16,722]{3,1,2,0:T(8,128)} fusion(bf16[320,16,361]{2,0,1:T(8,128)(2,1)S(1)} %get-tuple-element.6, bf16[320,16,361]{2,0,1:T(8,128)(2,1)S(1)} %get-tuple-element.5), kind=kOutput, calls=%fused_computation.12 | convolution fusion | flops 2381762560 | bytes 22179840 | tf_op jit(solution)/shard_map/gh,shck->sgck/dot_general | solution.py:65
  250.3 12.4 %convolution_bitcast_fusion = f32[1,320,16,722]{3,1,2,0:T(8,128)} fusion(bf16[320,16,361]{2,0,1:T(8,128)(2,1)S(1)} %get-tuple-element.6, bf16[320,16,361]{2,0,1:T(8,128)(2,1)S(1)} %get-tuple-element.5), kind=kOutput, calls=%fused_computation.11 | convolution fusion | flops 2381762560 | bytes 22179840 | tf_op jit(solution)/shard_map/gh,shck->sgck/dot_general | solution.py:66
  262.7 13.7 %fusion.10 = (bf16[1,320,16,361]{3,1,2,0:T(8,128)(2,1)S(1)}, bf16[1,320,16,361]{3,1,2,0:T(8,128)(2,1)S(1)}) fusion(f32[1,320,16,722]{3,1,2,0:T(8,128)} %convolution_bitcast_fusion, f32[1,320,16,722]{3,1,2,0:T(8,128)} %convolution_bitcast_fusion.1), kind=kLoop, calls=%fused_computation.18 | loop fusion | flops 7393280 | bytes 36966400 | tf_op jit(solution)/shard_map/convert.3
  282.5 8.4 %pad_maximum_fusion.1 = bf16[320,4,1,4,722]{4,3,1,2,0:T(4,128)(2,1)} fusion(bf16[320,4,1,4,361]{4,3,1,2,0:T(4,128)(2,1)S(1)} %copy.23, bf16[320,4,1,4,361]{4,3,1,2,0:T(4,128)(2,1)S(1)} %copy.22), kind=kLoop, calls=%fused_computation.24 | loop fusion | flops 14786560 | bytes 14786560 | tf_op jit(solution)/shard_map/concatenate | solution.py:67
  290.9 7.7 %all-to-all-start.1 = ((bf16[320,4,1,4,722]{4,3,1,2,0:T(4,128)(2,1)}), bf16[320,4,1,4,722]{4,3,1,2,0:T(4,128)(2,1)}, u32[]{:S(2)}, u32[]{:S(2)}) async-start(bf16[320,4,1,4,722]{4,3,1,2,0:T(4,128)(2,1)} %pad_maximum_fusion.1), calls=%async_computation.1 | async-start | bytes 15728640 | tf_op jit(solution)/shard_map/all_to_all | solution.py:104
  298.6 4.6 %sine_multiply_fusion = (f32[361,720]{0,1:T(8,128)S(1)}, f32[361,720]{0,1:T(8,128)S(1)}) fusion(f32[361]{0:T(512)S(1)} %fusion.57, f32[361]{0:T(512)S(1)} %fusion.56), kind=kLoop, calls=%fused_computation.58 | loop fusion | flops 2859120 | bytes 2082248 | tf_op jit(solution)/shard_map/mul | solution.py:25
  303.2 110.0 %all-to-all-done.1 = bf16[320,4,1,4,722]{4,3,1,2,0:T(4,128)(2,1)} async-done(((bf16[320,4,1,4,722]{4,3,1,2,0:T(4,128)(2,1)}), bf16[320,4,1,4,722]{4,3,1,2,0:T(4,128)(2,1)}, u32[]{:S(2)}, u32[]{:S(2)}) %all-to-all-start.1) | async-done | bytes 7393312 | tf_op jit(solution)/shard_map/all_to_all | solution.py:104
  413.2 10.6 %copy.24 = bf16[10,4,32,1,4,722]{5,4,2,1,0,3:T(4,128)(2,1)} copy(bf16[10,4,32,1,4,722]{5,4,1,0,2,3:T(4,128)(2,1)} %bitcast.26) | data formatting | bytes 14786560 | tf_op jit(solution)/shard_map/all_to_all | solution.py:104
  423.8 13.3 %reshape.106 = bf16[10,512,722]{2,1,0:T(8,128)(2,1)} reshape(bf16[10,4,32,1,4,722]{5,4,2,1,0,3:T(4,128)(2,1)} %copy.24) | data formatting | bytes 14786560 | tf_op jit(solution)/shard_map/reshape | solution.py:104
  437.1 12.5 %fusion.22 = bf16[1,10,720,512]{3,2,1,0:T(8,128)(2,1)} fusion(bf16[10,512,722]{2,1,0:T(8,128)(2,1)} %reshape.106, bf16[1,10,720,512]{3,2,1,0:T(8,128)(2,1)} %param.4, f32[361,720]{0,1:T(8,128)S(1)} %get-tuple-element.11, f32[361,720]{0,1:T(8,128)S(1)} %get-tuple-element.12), kind=kOutput, calls=%fused_computation.35 | convolution fusion | flops 5335780352 | bytes 24218240 | tf_op jit(solution)/shard_map/rck,kw->rwc/dot_general | solution.py:107
  (20 shorter events, 6.2 us)
Async XLA Ops:
  6.5 13.0 %slice-start = ((s8[7372800]{0:T(1024)(128)(4,1)}), s8[3178496]{0:T(1024)(128)(4,1)S(1)}, s32[]{:S(2)}) async-start(s8[7372800]{0:T(1024)(128)(4,1)} %bitcast.99), calls=%async_computation.3 | async-start | bytes 6356992
  6.5 202.1 %all-gather.2.cloned.1.call-start = ((), (), s32[]{:S(2)}) async-start(), calls=%async_computation.2 | async-start | bytes 9830400 | tf_op jit(solution)/shard_map/all_gather | solution.py:97
  10.7 8.9 %slice-start.1 = ((s8[7372800]{0:T(1024)(128)(4,1)}), s8[4194304]{0:T(1024)(128)(4,1)S(1)}, s32[]{:S(2)}) async-start(s8[7372800]{0:T(1024)(128)(4,1)} %bitcast.99), calls=%async_computation.4 | async-start | bytes 8388608
  15.3 7.7 %copy-start.1 = (f32[512]{0:T(512)S(1)}, f32[512]{0:T(512)}, u32[]{:S(2)}) copy-start(f32[512]{0:T(512)} %param.6) | copy-start | bytes 6148
  15.3 7.7 %copy-start.2 = (f32[512]{0:T(512)S(1)}, f32[512]{0:T(512)}, u32[]{:S(2)}) copy-start(f32[512]{0:T(512)} %param.5) | copy-start | bytes 6148
  181.9 15.1 %copy-start = (bf16[320,16,722]{2,1,0:T(8,128)(2,1)S(1)}, bf16[320,16,722]{2,1,0:T(8,128)(2,1)}, u32[]{:S(2)}) copy-start(bf16[320,16,722]{2,1,0:T(8,128)(2,1)} %reshape.105) | copy-start | bytes 22179844
  290.9 122.3 %all-to-all-start.1 = ((bf16[320,4,1,4,722]{4,3,1,2,0:T(4,128)(2,1)}), bf16[320,4,1,4,722]{4,3,1,2,0:T(4,128)(2,1)}, u32[]{:S(2)}, u32[]{:S(2)}) async-start(bf16[320,4,1,4,722]{4,3,1,2,0:T(4,128)(2,1)} %pad_maximum_fusion.1), calls=%async_computation.1 | async-start | bytes 15728640 | tf_op jit(solution)/shard_map/all_to_all | solution.py:104
Sparse Core Ops, SparseCore 0:
  10.8 60.0 all-gather.1
where the time goes:
time: 464 us; the launch traced here: 457 us
  waiting for transfers between devices  110 us (24%)
  blocking collectives  98.7 us (21%)
  local copies, waits for them, and re-layouts  82.3 us (18%)
  matrix products  75.8 us (16%)
  other arithmetic  68.4 us (15%)
  between operations  14 us (3%)
  starting transfers between devices  7.71 us (2%)
    all_to_all x1, waiting for transfers between devices, shards(): lax.all_to_all(back, 'space', split_axis=0, concat_axis=2, tiled=True)  110 us
    all_to_all x1, blocking collectives, shards(): lax.all_to_all(pieces, 'space', split_axis=2, concat_axis=0, tiled=True)  98.7 us
    reshape x2, local copies, waits for them, and re-layouts, shards(): rowspec.reshape(row_count, dp_count, space_count, chan_part, spec_len)  24.4 us
    concatenate x1, other arithmetic, filter_inverse(): jnp.concatenate([spec_re * filt_re - spec_im * filt_im, spec_re * filt_im...  18.9 us
    dot_general x1, matrix products, column_forward(): jnp.einsum('gh,shck->sgck', col_sine, slab, preferred_element_type=jnp.fl...  15.1 us
    another operation x1, other arithmetic  13.7 us
    another operation x1, local copies, waits for them, and re-layouts  13.3 us
    reshape x1, local copies, waits for them, and re-layouts, shards(): lax.all_to_all(back, 'space', split_axis=0, concat_axis=2, tiled=True)  13.3 us
  transfers between devices with their start and end apart: 2, of which 1 were waited for; matrix products, arithmetic and copies ran while one was open for 23% of the time, Pallas kernels for 0%

commit v1 on v0

v1 whole, which is shorter than its diff:
```python
import functools
import math

import jax
import jax.numpy as jnp
import ml_dtypes
import numpy as np
from jax import lax
from jax.experimental import pallas as pl
from jax.experimental.pallas import tpu as pltpu
from jax.sharding import PartitionSpec as P

BOTH = ("dp", "space")
WIDE = 384
HALF = WIDE // 2
MIB = 1024 * 1024


def chunk_starts(freqs):
    return range(0, freqs, HALF)


def lane_layout(start, freqs):
    lane = np.arange(WIDE)
    tail = lane >= 256
    imag = np.where(tail, lane >= 320, lane >= 128)
    freq = start + np.where(tail, 128 + lane % 64, lane % 128)
    return np.minimum(freq, freqs - 1), imag, freq < freqs


def row_tables(lon_len, start):
    freqs = lon_len // 2 + 1
    freq, imag, used = lane_layout(start, freqs)
    lon = np.arange(lon_len)
    turns = (lon[:, None] * freq[None, :] % lon_len).astype(np.float32) * np.float32(
        2.0 * math.pi / lon_len
    )
    scale = np.float32(1.0 / math.sqrt(lon_len))
    wave = np.where(imag, -np.sin(turns), np.cos(turns)) * used
    weight = np.where((freq == 0) | (freq == lon_len // 2), 1.0, 2.0).astype(np.float32)
    forward = (wave * scale).astype(ml_dtypes.bfloat16)
    inverse = (wave * weight * scale).astype(ml_dtypes.bfloat16)
    return forward, inverse


def column_tables(lat_len, chan_part):
    lat = np.arange(lat_len)
    turns = (lat[:, None] * lat[None, :] % lat_len).astype(np.float32) * np.float32(
        2.0 * math.pi / lat_len
    )
    scale = np.float32(1.0 / math.sqrt(lat_len))
    size = chan_part * lat_len
    forward = np.zeros((chan_part, lat_len, 2, lat_len, chan_part), np.float32)
    for chan in range(chan_part):
        forward[chan, :, 0, :, chan] = np.cos(turns) * scale
        forward[chan, :, 1, :, chan] = np.sin(turns) * scale
    inverse = forward.transpose(3, 4, 2, 0, 1).reshape(size, 2 * size)
    forward = forward.reshape(size, 2 * size)
    return forward.astype(ml_dtypes.bfloat16), inverse.astype(ml_dtypes.bfloat16)


def swap_parts(values):
    tail = values[:, 256:]
    return jnp.concatenate(
        [values[:, 128:256], values[:, :128], pltpu.roll(tail, 64, axis=1)], axis=1
    )


def imag_lanes(shape):
    lane = lax.broadcasted_iota(jnp.int32, shape, len(shape) - 1)
    return ((lane >= 128) & (lane < 256)) | (lane >= 320)


def first_half(shape):
    return lax.broadcasted_iota(jnp.int32, shape, 1) < 4


def pre_kernel(x_ref, gain_ref, bias_ref, table_ref, out_ref):
    specs = []
    for row in range(2):
        wide = x_ref[row].astype(jnp.float32)
        center = jnp.mean(wide, axis=-1, keepdims=True)
        wide = wide - center
        spread = jnp.mean(jnp.square(wide), axis=-1, keepdims=True)
        normed = (wide * lax.rsqrt(spread + 1e-05) * gain_ref[...] + bias_ref[...]).astype(
            jnp.bfloat16
        )
        spec = lax.dot_general(
            normed, table_ref[...], (((0,), (0,)), ((), ())), preferred_element_type=jnp.float32
        )
        specs.append(spec.reshape(spec.shape[0] // 8, 8, WIDE))
    top = first_half(specs[0].shape)
    low = jnp.where(top, specs[0], pltpu.roll(specs[1], 4, axis=1)).astype(jnp.bfloat16)
    high = jnp.where(top, pltpu.roll(specs[0], 4, axis=1), specs[1]).astype(jnp.bfloat16)
    out_ref[:, 0, 0] = low
    out_ref[:, 1, 0] = high


def pre(grid, gain, bias, table):
    rows, lon_len, channels = grid.shape
    out = pl.pallas_call(
        pre_kernel,
        grid=(rows // 2,),
        in_specs=[
            pl.BlockSpec((2, lon_len, channels), lambda i: (i, 0, 0)),
            pl.BlockSpec((1, channels), lambda i: (0, 0)),
            pl.BlockSpec((1, channels), lambda i: (0, 0)),
            pl.BlockSpec((lon_len, WIDE), lambda i: (0, 0)),
        ],
        out_specs=pl.BlockSpec((channels // 8, 2, 1, 8, WIDE), lambda i: (0, 0, i, 0, 0)),
        out_shape=jax.ShapeDtypeStruct((channels // 8, 2, rows // 2, 8, WIDE), jnp.bfloat16),
        compiler_params=pltpu.CompilerParams(vmem_limit_bytes=40 * MIB),
        cost_estimate=pl.CostEstimate(
            flops=2 * rows * lon_len * channels * WIDE,
            bytes_accessed=2 * rows * channels * (lon_len + WIDE),
            transcendentals=rows * lon_len,
        ),
        name="row_forward",
    )(grid, gain, bias, table)
    return out.reshape(channels // 4, rows // 2, 8, WIDE)


def mid_kernel(x_ref, filt_ref, forward_ref, inverse_ref, out_ref, x_both, mixed):
    size = x_both.shape[0] // 2
    rows = x_ref[...].astype(jnp.float32).reshape(size, WIDE)
    imag = imag_lanes(rows.shape)
    turned = swap_parts(rows)
    x_both[:size] = rows.astype(jnp.bfloat16)
    x_both[size:] = jnp.where(imag, -turned, turned).astype(jnp.bfloat16)
    lat_len = size // 4
    for chan in range(4):
        part = pl.ds(chan * lat_len, lat_len)
        spec = jnp.dot(forward_ref[part], x_both[...], preferred_element_type=jnp.float32)
        both = filt_ref[0, part] * spec + filt_ref[1, part] * swap_parts(spec)
        turned = swap_parts(both)
        mixed[part] = both.astype(jnp.bfloat16)
        mixed[pl.ds(size + chan * lat_len, lat_len)] = jnp.where(
            imag_lanes(both.shape), turned, -turned
        ).astype(jnp.bfloat16)
    back = jnp.dot(inverse_ref[...], mixed[...], preferred_element_type=jnp.float32)
    out_ref[...] = back.reshape(out_ref.shape).astype(jnp.bfloat16)


def mid(slab, filt, forward, inverse, samples):
    devices, pairs, eight, _ = slab.shape
    spaces = devices // samples
    size = spaces * pairs * eight
    block = pl.BlockSpec((spaces, pairs, eight, WIDE), lambda s: (s, 0, 0, 0))
    return pl.pallas_call(
        mid_kernel,
        grid=(samples,),
        in_specs=[
            block,
            pl.BlockSpec((2, size, WIDE), lambda s: (0, 0, 0)),
            pl.BlockSpec((size, 2 * size), lambda s: (0, 0)),
            pl.BlockSpec((size, 2 * size), lambda s: (0, 0)),
        ],
        out_specs=block,
        out_shape=jax.ShapeDtypeStruct(slab.shape, jnp.bfloat16),
        scratch_shapes=[
            pltpu.VMEM((2 * size, WIDE), jnp.bfloat16),
            pltpu.VMEM((2 * size, WIDE), jnp.bfloat16),
        ],
        compiler_params=pltpu.CompilerParams(vmem_limit_bytes=56 * MIB),
        cost_estimate=pl.CostEstimate(
            flops=samples * 8 * size * size * WIDE,
            bytes_accessed=4 * samples * size * WIDE + 8 * size * (WIDE + size),
            transcendentals=0,
        ),
        name="columns",
    )(slab, filt, forward, inverse)


def post_kernel(back_ref, x_ref, table_ref, out_ref):
    first = back_ref[:, 0, 0].astype(jnp.float32)
    second = back_ref[:, 1, 0].astype(jnp.float32)
    top = first_half(first.shape)
    rows = (
        jnp.where(top, first, pltpu.roll(second, 4, axis=1)),
        jnp.where(top, pltpu.roll(first, 4, axis=1), second),
    )
    for row in range(2):
        spec = rows[row].reshape(first.shape[0] * 8, WIDE).astype(jnp.bfloat16)
        branch = lax.dot_general(
            table_ref[...], spec, (((1,), (1,)), ((), ())), preferred_element_type=jnp.float32
        )
        out_ref[row] = (x_ref[row].astype(jnp.float32) + branch).astype(jnp.bfloat16)


def post(back, grid, table):
    rows, lon_len, channels = grid.shape
    block = pl.BlockSpec((2, lon_len, channels), lambda i: (i, 0, 0))
    return pl.pallas_call(
        post_kernel,
        grid=(rows // 2,),
        in_specs=[
            pl.BlockSpec((channels // 8, 2, 1, 8, WIDE), lambda i: (0, 0, i, 0, 0)),
            block,
            pl.BlockSpec((lon_len, WIDE), lambda i: (0, 0)),
        ],
        out_specs=block,
        out_shape=jax.ShapeDtypeStruct(grid.shape, jnp.bfloat16),
        compiler_params=pltpu.CompilerParams(vmem_limit_bytes=40 * MIB),
        cost_estimate=pl.CostEstimate(
            flops=2 * rows * lon_len * channels * WIDE,
            bytes_accessed=2 * rows * channels * (2 * lon_len + WIDE),
            transcendentals=0,
        ),
        name="row_inverse",
    )(back.reshape(channels // 8, 2, rows // 2, 8, WIDE), grid, table)


def filter_chunk(filt, start):
    freqs = filt.shape[-1] // 2
    by_chan = filt.transpose(1, 0, 2).reshape(-1, 2 * freqs)

    def lanes(first):
        stop = min(start + HALF, freqs)
        taken = by_chan[:, first + start : first + stop]
        return jnp.pad(taken, ((0, 0), (0, HALF - taken.shape[1])))

    real, imag = lanes(0), lanes(freqs)

    def lay(one, two):
        return jnp.concatenate([one[:, :128], two[:, :128], one[:, 128:], two[:, 128:]], axis=1)

    return jnp.stack([lay(real, real), lay(-imag, imag)])


def swap_devices(blocks):
    return lax.all_to_all(blocks, BOTH, split_axis=0, concat_axis=0, tiled=True)


def shards(samples, norm_gain, norm_bias, spectral_filter):
    grid = samples[0]
    rows, lon_len, channels = grid.shape
    dp_count = lax.axis_size("dp")
    lat_len = rows * lax.axis_size("space")
    starts = chunk_starts(lon_len // 2 + 1)
    tables = [row_tables(lon_len, start) for start in starts]
    forward, inverse = column_tables(lat_len, spectral_filter.shape[1])
    gain, bias = norm_gain[None], norm_bias[None]
    slabs = [swap_devices(pre(grid, gain, bias, jnp.asarray(table[0]))) for table in tables]
    backs = [
        swap_devices(
            mid(
                slab,
                filter_chunk(spectral_filter, start),
                jnp.asarray(forward),
                jnp.asarray(inverse),
                dp_count,
            )
        )
        for slab, start in zip(slabs, starts)
    ]
    for back, table in zip(backs, tables):
        grid = post(back, grid, jnp.asarray(table[1]))
    return grid[None]


def solution(mesh):
    placed = (P("dp", "space", None, None), P(), P(), P(None, BOTH, None))
    return jax.shard_map(
        shards, mesh=mesh, in_specs=placed, out_specs=P("dp", "space", None, None), check_vma=False
    )
```

time: 464 us -> 257 us (0.55)
  Pallas kernels: 0 us -> 108 us
  blocking collectives: 98.7 us -> 0 us
  matrix products: 75.8 us -> 0 us
  other arithmetic: 68.4 us -> 8.14 us
  local copies, waits for them, and re-layouts: 82.3 us -> 24.4 us
  waiting for transfers between devices: 110 us -> 78.5 us
  starting transfers between devices: 7.71 us -> 34.1 us
  between operations: 14 us -> 0.24 us
    pallas_call x0 -> x6, Pallas kernels: none -> 108 us  [the longest x2 70.1 us: mid(): pl.pallas_call(mid_kernel, grid=(samples,), in_specs=[block, pl.BlockSpec...]
    all_to_all x1 -> x0, blocking collectives: 98.7 us -> none  [shards(): lax.all_to_all(pieces, 'space', split_axis=2, concat_axis=0, tiled=True)]
    dot_general x6 -> x0, matrix products: 75.8 us -> none  [the longest x1 15.1 us: column_forward(): jnp.einsum('gh,shck->sgck', col_sine, slab, preferred_element_type=jnp.fl...]
    reshape x3 -> x0, local copies, waits for them, and re-layouts: 37.7 us -> none  [the longest x2 24.4 us: shards(): rowspec.reshape(row_count, dp_count, space_count, chan_part, spec_len)]
    all_to_all x1 -> x4, waiting for transfers between devices: 110 us -> 78.5 us  [swap_devices(): return lax.all_to_all(blocks, BOTH, split_axis=0, concat_axis=0, tiled=True)]
    concatenate x2 -> x0, other arithmetic: 27.3 us -> none  [the longest x1 18.9 us: filter_inverse(): jnp.concatenate([spec_re * filt_re - spec_im * filt_im, spec_re * filt_im...]
    all_to_all x1 -> x4, starting transfers between devices: 7.71 us -> 34.1 us  [swap_devices(): return lax.all_to_all(blocks, BOTH, split_axis=0, concat_axis=0, tiled=True)]
    another operation x1 -> x0, local copies, waits for them, and re-layouts: 13.3 us -> none
  transfers between devices with their start and end apart: 2 -> 4, of which waited for: 1 -> 4; matrix products, arithmetic and copies ran while one was open for 23% -> 7% of each run, Pallas kernels for 0% -> 35%
where the time goes in v1:
time: 257 us; the launch traced here: 254 us
  Pallas kernels  108 us (42%)
  waiting for transfers between devices  78.5 us (31%)
  starting transfers between devices  34.1 us (13%)
  local copies, waits for them, and re-layouts  24.4 us (9%)
  other arithmetic  8.14 us (3%)
    all_to_all x4, waiting for transfers between devices, swap_devices(): return lax.all_to_all(blocks, BOTH, split_axis=0, concat_axis=0, tiled=True)  78.5 us
    pallas_call x2, Pallas kernels, mid(): pl.pallas_call(mid_kernel, grid=(samples,), in_specs=[block, pl.BlockSpec...  70.1 us
    all_to_all x4, starting transfers between devices, swap_devices(): return lax.all_to_all(blocks, BOTH, split_axis=0, concat_axis=0, tiled=True)  34.1 us
    pallas_call x2, Pallas kernels, pre(): pl.pallas_call(pre_kernel, grid=(rows // 2,), in_specs=[pl.BlockSpec((2,...  21.6 us
    pallas_call x2, Pallas kernels, post(): pl.pallas_call(post_kernel, grid=(rows // 2,), in_specs=[pl.BlockSpec((ch...  16.6 us
    unnamed x32, local copies, waits for them, and re-layouts  15.9 us
    another operation x5, other arithmetic, filter_chunk(): return jnp.stack([lay(real, real), lay(-imag, imag)])  5.44 us
  transfers between devices with their start and end apart: 4, of which 4 were waited for; matrix products, arithmetic and copies ran while one was open for 7% of the time, Pallas kernels for 35%

profile of v1, /device:TPU:14, one launch (start us, length us, event | category | flops | bytes accessed | tf_op | source)
XLA Modules:
  0.0 253.8 jit_solution(13672954422805836172)
XLA Ops:
  0.0 3.1 %copy-done = bf16[1,10,720,512]{3,2,1,0:T(8,128)(2,1)S(1)} copy-done((bf16[1,10,720,512]{3,2,1,0:T(8,128)(2,1)S(1)}, bf16[1,10,720,512]{3,2,1,0:T(8,128)(2,1)}, u32[]{:S(2)}) %copy-start) | copy-done | bytes 7372824
  5.5 10.8 %row_forward.3 = bf16[64,2,5,8,384]{4,3,2,1,0:T(8,128)(2,1)S(1)} custom-call(bf16[10,720,512]{2,1,0:T(8,128)(2,1)S(1)} %bitcast.19, f32[1,512]{1,0:T(1,128)S(1)} %bitcast.25, f32[1,512]{1,0:T(1,128)S(1)} %bitcast.27, bf16[720,384]{1,0:T(8,128)(2,1)S(1)} %copy-done.8), custom_call_target="tpu_custom_call" | custom-call | flops 2831155200 | bytes 11304960 | tf_op jit(solution)/shard_map/row_forward/pallas_call | solution.py:101
  16.3 1.9 copy-done.4
  18.2 10.8 %all-to-all-start.2 = ((bf16[128,5,8,384]{3,2,1,0:T(8,128)(2,1)}), bf16[128,5,8,384]{3,2,1,0:T(8,128)(2,1)}, u32[]{:S(2)}, u32[]{:S(2)}) async-start(bf16[128,5,8,384]{3,2,1,0:T(8,128)(2,1)} %bitcast.24), calls=%async_computation.2 | async-start | bytes 7864320 | tf_op jit(solution)/shard_map/all_to_all | solution.py:231
  29.0 4.9 %copy.11 = f32[4,320,722]{2,1,0:T(8,128)} copy(f32[4,320,722]{2,0,1:T(4,128)} %bitcast.33) | data formatting | bytes 7393280 | tf_op jit(solution)/shard_map/transpose | solution.py:215
  34.0 10.8 %row_forward.2 = bf16[64,2,5,8,384]{4,3,2,1,0:T(8,128)(2,1)S(1)} custom-call(bf16[10,720,512]{2,1,0:T(8,128)(2,1)S(1)} %bitcast.22, f32[1,512]{1,0:T(1,128)S(1)} %bitcast.26, f32[1,512]{1,0:T(1,128)S(1)} %bitcast.28, bf16[720,384]{1,0:T(8,128)(2,1)S(1)} %copy-done.7), custom_call_target="tpu_custom_call" | custom-call | flops 2831155200 | bytes 11304960 | tf_op jit(solution)/shard_map/row_forward/pallas_call | solution.py:101
  44.8 1.9 copy-done.3
  46.7 29.7 %all-to-all-done.2.x_ref = bf16[128,5,8,384]{3,2,1,0:T(8,128)(2,1)} async-done(((bf16[128,5,8,384]{3,2,1,0:T(8,128)(2,1)}), bf16[128,5,8,384]{3,2,1,0:T(8,128)(2,1)}, u32[]{:S(2)}, u32[]{:S(2)}) %all-to-all-start.2) | async-done | bytes 3932192 | tf_op jit(solution)/shard_map/all_to_all | solution.py:231
  76.4 7.8 %all-to-all-start = ((bf16[128,5,8,384]{3,2,1,0:T(8,128)(2,1)}), bf16[128,5,8,384]{3,2,1,0:T(8,128)(2,1)}, u32[]{:S(2)}, u32[]{:S(2)}) async-start(bf16[128,5,8,384]{3,2,1,0:T(8,128)(2,1)} %bitcast.23), calls=%async_computation | async-start | bytes 7864320 | tf_op jit(solution)/shard_map/all_to_all | solution.py:231
  84.2 2.5 fusion.2
  88.6 2.1 pad_maximum_fusion.1.filt_ref
  90.8 35.1 %columns.3 = bf16[128,5,8,384]{3,2,1,0:T(8,128)(2,1)} custom-call(bf16[128,5,8,384]{3,2,1,0:T(8,128)(2,1)} %all-to-all-done.2.x_ref, f32[2,1280,384]{2,1,0:T(8,128)} %pad_maximum_fusion.1.filt_ref, bf16[1280,2560]{1,0:T(8,128)(2,1)} %constant.17.clone.forward_ref, bf16[1280,2560]{1,0:T(8,128)(2,1)} %constant.18.clone.inverse_ref), custom_call_target="tpu_custom_call" | custom-call | flops 20132659200 | bytes 24903680 | tf_op jit(solution)/shard_map/columns/pallas_call | solution.py:149
  125.8 5.8 %all-to-all-done.x_ref = bf16[128,5,8,384]{3,2,1,0:T(8,128)(2,1)} async-done(((bf16[128,5,8,384]{3,2,1,0:T(8,128)(2,1)}), bf16[128,5,8,384]{3,2,1,0:T(8,128)(2,1)}, u32[]{:S(2)}, u32[]{:S(2)}) %all-to-all-start) | async-done | bytes 3932192 | tf_op jit(solution)/shard_map/all_to_all | solution.py:231
  131.6 7.8 %all-to-all-start.3 = ((bf16[128,5,8,384]{3,2,1,0:T(8,128)(2,1)}), bf16[128,5,8,384]{3,2,1,0:T(8,128)(2,1)}, u32[]{:S(2)}, u32[]{:S(2)}) async-start(bf16[128,5,8,384]{3,2,1,0:T(8,128)(2,1)} %columns.3), calls=%async_computation.3 | async-start | bytes 7864320 | tf_op jit(solution)/shard_map/all_to_all | solution.py:231
  139.4 2.6 %fusion.4 = (f32[1280,169]{1,0:T(8,128)S(1)}, f32[1280,169]{1,0:T(8,128)S(1)}) fusion(f32[1280,722]{1,0:T(8,128)} %bitcast.30), kind=kLoop, calls=%fused_computation.15 | loop fusion | bytes 3461120 | tf_op jit(solution)/shard_map/slice | solution.py:219
  142.9 2.2 pad_maximum_fusion.filt_ref
  145.0 35.1 %columns.2 = bf16[128,5,8,384]{3,2,1,0:T(8,128)(2,1)} custom-call(bf16[128,5,8,384]{3,2,1,0:T(8,128)(2,1)} %all-to-all-done.x_ref, f32[2,1280,384]{2,1,0:T(8,128)} %pad_maximum_fusion.filt_ref, bf16[1280,2560]{1,0:T(8,128)(2,1)} %constant.17.clone.forward_ref, bf16[1280,2560]{1,0:T(8,128)(2,1)} %constant.18.clone.inverse_ref), custom_call_target="tpu_custom_call" | custom-call | flops 20132659200 | bytes 24903680 | tf_op jit(solution)/shard_map/columns/pallas_call | solution.py:149
  180.1 6.7 %all-to-all-done.3 = bf16[128,5,8,384]{3,2,1,0:T(8,128)(2,1)} async-done(((bf16[128,5,8,384]{3,2,1,0:T(8,128)(2,1)}), bf16[128,5,8,384]{3,2,1,0:T(8,128)(2,1)}, u32[]{:S(2)}, u32[]{:S(2)}) %all-to-all-start.3) | async-done | bytes 3932192 | tf_op jit(solution)/shard_map/all_to_all | solution.py:231
  186.8 7.8 %all-to-all-start.1 = ((bf16[128,5,8,384]{3,2,1,0:T(8,128)(2,1)}), bf16[128,5,8,384]{3,2,1,0:T(8,128)(2,1)}, u32[]{:S(2)}, u32[]{:S(2)}) async-start(bf16[128,5,8,384]{3,2,1,0:T(8,128)(2,1)} %columns.2), calls=%async_computation.1 | async-start | bytes 7864320 | tf_op jit(solution)/shard_map/all_to_all | solution.py:231
  194.6 8.0 %row_inverse.2.x_ref = bf16[10,720,512]{2,1,0:T(8,128)(2,1)S(1)} custom-call(bf16[64,2,5,8,384]{4,3,2,1,0:T(8,128)(2,1)} %bitcast.12.back_ref, bf16[10,720,512]{2,1,0:T(8,128)(2,1)} %bitcast.18, bf16[720,384]{1,0:T(8,128)(2,1)S(1)} %copy-done.6), custom_call_target="tpu_custom_call" | custom-call | flops 2831155200 | bytes 18677760 | tf_op jit(solution)/shard_map/row_inverse/pallas_call | solution.py:193
  202.6 3.0 %copy-done.1 = bf16[10,720,512]{2,1,0:T(8,128)(2,1)} copy-done((bf16[10,720,512]{2,1,0:T(8,128)(2,1)}, bf16[10,720,512]{2,1,0:T(8,128)(2,1)S(1)}, u32[]{:S(2)}) %copy-start.1) | copy-done | bytes 7372824
  205.7 36.4 %all-to-all-done.1 = bf16[128,5,8,384]{3,2,1,0:T(8,128)(2,1)} async-done(((bf16[128,5,8,384]{3,2,1,0:T(8,128)(2,1)}), bf16[128,5,8,384]{3,2,1,0:T(8,128)(2,1)}, u32[]{:S(2)}, u32[]{:S(2)}) %all-to-all-start.1) | async-done | bytes 3932192 | tf_op jit(solution)/shard_map/all_to_all | solution.py:231
  242.0 3.1 %copy-done.2 = bf16[10,720,512]{2,1,0:T(8,128)(2,1)S(1)} copy-done((bf16[10,720,512]{2,1,0:T(8,128)(2,1)S(1)}, bf16[10,720,512]{2,1,0:T(8,128)(2,1)}, u32[]{:S(2)}) %copy-start.2) | copy-done | bytes 7372824
  245.1 8.6 %row_inverse.3 = bf16[10,720,512]{2,1,0:T(8,128)(2,1)} custom-call(bf16[64,2,5,8,384]{4,3,2,1,0:T(8,128)(2,1)} %bitcast.8.back_ref, bf16[10,720,512]{2,1,0:T(8,128)(2,1)S(1)} %copy-done.2, bf16[720,384]{1,0:T(8,128)(2,1)S(1)} %copy-done.5), custom_call_target="tpu_custom_call" | custom-call | flops 2831155200 | bytes 18677760 | tf_op jit(solution)/shard_map/row_inverse/pallas_call | solution.py:193
  (37 shorter events, 5.1 us)
Async XLA Ops:
  0.0 3.1 %copy-start = (bf16[1,10,720,512]{3,2,1,0:T(8,128)(2,1)S(1)}, bf16[1,10,720,512]{3,2,1,0:T(8,128)(2,1)}, u32[]{:S(2)}) copy-start(bf16[1,10,720,512]{3,2,1,0:T(8,128)(2,1)} %param.10) | copy-start | bytes 22118404
  3.1 1.1 copy-start.8
  4.1 0.7 copy-start.9
  4.8 0.7 copy-start.11
  16.3 1.9 copy-start.4
  18.2 15.7 %slice-start = ((s8[7372800]{0:T(1024)(128)(4,1)}), s8[3178496]{0:T(1024)(128)(4,1)S(1)}, s32[]{:S(2)}) async-start(s8[7372800]{0:T(1024)(128)(4,1)} %bitcast.20), calls=%async_computation.4 | async-start | bytes 6356992
  18.2 58.2 %all-to-all-start.2 = ((bf16[128,5,8,384]{3,2,1,0:T(8,128)(2,1)}), bf16[128,5,8,384]{3,2,1,0:T(8,128)(2,1)}, u32[]{:S(2)}, u32[]{:S(2)}) async-start(bf16[128,5,8,384]{3,2,1,0:T(8,128)(2,1)} %bitcast.24), calls=%async_computation.2 | async-start | bytes 7864320 | tf_op jit(solution)/shard_map/all_to_all | solution.py:231
  29.0 5.0 %slice-start.1 = ((s8[7372800]{0:T(1024)(128)(4,1)}), s8[4194304]{0:T(1024)(128)(4,1)S(1)}, s32[]{:S(2)}) async-start(s8[7372800]{0:T(1024)(128)(4,1)} %bitcast.20), calls=%async_computation.5 | async-start | bytes 8388608
  29.0 5.0 %copy-start.7 = (bf16[720,384]{1,0:T(8,128)(2,1)S(1)}, bf16[720,384]{1,0:T(8,128)(2,1)}, u32[]{:S(2)}) copy-start(bf16[720,384]{1,0:T(8,128)(2,1)} %constant.16.clone.table_ref) | copy-start | bytes 1658884
  29.0 5.0 %copy-start.10 = (f32[512]{0:T(512)S(1)}, f32[512]{0:T(512)}, u32[]{:S(2)}) copy-start(f32[512]{0:T(512)} %param.11) | copy-start | bytes 6148
  29.0 5.0 %copy-start.12 = (f32[512]{0:T(512)S(1)}, f32[512]{0:T(512)}, u32[]{:S(2)}) copy-start(f32[512]{0:T(512)} %param.12) | copy-start | bytes 6148
  44.8 1.9 copy-start.3
  76.4 55.2 %all-to-all-start = ((bf16[128,5,8,384]{3,2,1,0:T(8,128)(2,1)}), bf16[128,5,8,384]{3,2,1,0:T(8,128)(2,1)}, u32[]{:S(2)}, u32[]{:S(2)}) async-start(bf16[128,5,8,384]{3,2,1,0:T(8,128)(2,1)} %bitcast.23), calls=%async_computation | async-start | bytes 7864320 | tf_op jit(solution)/shard_map/all_to_all | solution.py:231
  84.2 3.1 %copy-start.13 = (f32[4,320,722]{2,1,0:T(8,128)S(1)}, f32[4,320,722]{2,1,0:T(8,128)}, u32[]{:S(2)}) copy-start(f32[4,320,722]{2,1,0:T(8,128)} %copy.11) | copy-start | bytes 11089924
  131.6 55.2 %all-to-all-start.3 = ((bf16[128,5,8,384]{3,2,1,0:T(8,128)(2,1)}), bf16[128,5,8,384]{3,2,1,0:T(8,128)(2,1)}, u32[]{:S(2)}, u32[]{:S(2)}) async-start(bf16[128,5,8,384]{3,2,1,0:T(8,128)(2,1)} %columns.3), calls=%async_computation.3 | async-start | bytes 7864320 | tf_op jit(solution)/shard_map/all_to_all | solution.py:231
  180.1 14.5 %copy-start.6 = (bf16[720,384]{1,0:T(8,128)(2,1)S(1)}, bf16[720,384]{1,0:T(8,128)(2,1)}, u32[]{:S(2)}) copy-start(bf16[720,384]{1,0:T(8,128)(2,1)} %constant.19.clone.table_ref) | copy-start | bytes 1658884
  186.8 55.2 %all-to-all-start.1 = ((bf16[128,5,8,384]{3,2,1,0:T(8,128)(2,1)}), bf16[128,5,8,384]{3,2,1,0:T(8,128)(2,1)}, u32[]{:S(2)}, u32[]{:S(2)}) async-start(bf16[128,5,8,384]{3,2,1,0:T(8,128)(2,1)} %columns.2), calls=%async_computation.1 | async-start | bytes 7864320 | tf_op jit(solution)/shard_map/all_to_all | solution.py:231
  194.6 47.4 %copy-start.5 = (bf16[720,384]{1,0:T(8,128)(2,1)S(1)}, bf16[720,384]{1,0:T(8,128)(2,1)}, u32[]{:S(2)}) copy-start(bf16[720,384]{1,0:T(8,128)(2,1)} %constant.20.clone.table_ref) | copy-start | bytes 1658884
  202.6 3.1 %copy-start.1 = (bf16[10,720,512]{2,1,0:T(8,128)(2,1)}, bf16[10,720,512]{2,1,0:T(8,128)(2,1)S(1)}, u32[]{:S(2)}) copy-start(bf16[10,720,512]{2,1,0:T(8,128)(2,1)S(1)} %row_inverse.2.x_ref) | copy-start | bytes 22118404
  242.0 3.1 %copy-start.2 = (bf16[10,720,512]{2,1,0:T(8,128)(2,1)S(1)}, bf16[10,720,512]{2,1,0:T(8,128)(2,1)}, u32[]{:S(2)}) copy-start(bf16[10,720,512]{2,1,0:T(8,128)(2,1)} %copy-done.1) | copy-start | bytes 22118404

commit v2 on v1

v2 whole, which is shorter than its diff:
```python
import functools
import math

import jax
import jax.numpy as jnp
import ml_dtypes
import numpy as np
from jax import lax
from jax.experimental import pallas as pl
from jax.experimental.pallas import tpu as pltpu
from jax.sharding import PartitionSpec as P

BOTH = ("dp", "space")
LANES = 128
FIRST = 256
MIB = 1024 * 1024
VMEM = 62 * MIB


def chunks(freqs):
    rest = -(-(freqs - FIRST) // LANES) * LANES
    return ((0, 2 * FIRST), (FIRST, 2 * rest))


def row_tables(lon_len, start, wide):
    freqs = lon_len // 2 + 1
    lane = np.arange(wide)
    imag = lane // LANES % 2 == 1
    freq = start + lane // (2 * LANES) * LANES + lane % LANES
    used = freq < freqs
    freq = np.minimum(freq, freqs - 1)
    lon = np.arange(lon_len)
    turns = (lon[:, None] * freq[None, :] % lon_len).astype(np.float32) * np.float32(
        2.0 * math.pi / lon_len
    )
    scale = np.float32(1.0 / math.sqrt(lon_len))
    wave = np.where(imag, -np.sin(turns), np.cos(turns)) * used
    weight = np.where((freq == 0) | (freq == lon_len // 2), 1.0, 2.0).astype(np.float32)
    forward = (wave * scale).astype(ml_dtypes.bfloat16)
    inverse = (wave * weight * scale).astype(ml_dtypes.bfloat16)
    return forward, inverse


def column_tables(lat_len, chan_part):
    lat = np.arange(lat_len)
    turns = (lat[:, None] * lat[None, :] % lat_len).astype(np.float32) * np.float32(
        2.0 * math.pi / lat_len
    )
    scale = np.float32(1.0 / math.sqrt(lat_len))
    size = chan_part * lat_len
    forward = np.zeros((chan_part, lat_len, 2, lat_len, chan_part), np.float32)
    for chan in range(chan_part):
        forward[chan, :, 0, :, chan] = np.cos(turns) * scale
        forward[chan, :, 1, :, chan] = np.sin(turns) * scale
    inverse = forward.transpose(3, 4, 2, 0, 1).reshape(size, 2 * size)
    forward = forward.reshape(size, 2 * size)
    return forward.astype(ml_dtypes.bfloat16), inverse.astype(ml_dtypes.bfloat16)


def swap_parts(values, sign=1):
    tiles = []
    for lane in range(0, values.shape[1], 2 * LANES):
        real = values[:, lane : lane + LANES]
        imag = values[:, lane + LANES : lane + 2 * LANES]
        tiles += [imag, -real] if sign > 0 else [-imag, real]
    return jnp.concatenate(tiles, axis=1)


def first_half(shape):
    return lax.broadcasted_iota(jnp.int32, shape, 1) < 4


def pre_kernel(x_ref, gain_ref, bias_ref, table_ref, out_ref):
    specs = []
    for row in range(2):
        wide = x_ref[row].astype(jnp.float32)
        center = jnp.mean(wide, axis=-1, keepdims=True)
        wide = wide - center
        spread = jnp.mean(jnp.square(wide), axis=-1, keepdims=True)
        normed = (wide * lax.rsqrt(spread + 1e-05) * gain_ref[...] + bias_ref[...]).astype(
            jnp.bfloat16
        )
        spec = lax.dot_general(
            normed, table_ref[...], (((0,), (0,)), ((), ())), preferred_element_type=jnp.float32
        )
        specs.append(spec.reshape(spec.shape[0] // 8, 8, spec.shape[1]))
    top = first_half(specs[0].shape)
    low = jnp.where(top, specs[0], pltpu.roll(specs[1], 4, axis=1)).astype(jnp.bfloat16)
    high = jnp.where(top, pltpu.roll(specs[0], 4, axis=1), specs[1]).astype(jnp.bfloat16)
    out_ref[:, 0, 0] = low
    out_ref[:, 1, 0] = high


def pre(grid, gain, bias, table):
    rows, lon_len, channels = grid.shape
    wide = table.shape[1]
    out = pl.pallas_call(
        pre_kernel,
        grid=(rows // 2,),
        in_specs=[
            pl.BlockSpec((2, lon_len, channels), lambda i: (i, 0, 0)),
            pl.BlockSpec((1, channels), lambda i: (0, 0)),
            pl.BlockSpec((1, channels), lambda i: (0, 0)),
            pl.BlockSpec((lon_len, wide), lambda i: (0, 0)),
        ],
        out_specs=pl.BlockSpec((channels // 8, 2, 1, 8, wide), lambda i: (0, 0, i, 0, 0)),
        out_shape=jax.ShapeDtypeStruct((channels // 8, 2, rows // 2, 8, wide), jnp.bfloat16),
        compiler_params=pltpu.CompilerParams(vmem_limit_bytes=VMEM),
        cost_estimate=pl.CostEstimate(
            flops=2 * rows * lon_len * channels * wide,
            bytes_accessed=2 * rows * channels * (lon_len + wide),
            transcendentals=rows * lon_len,
        ),
        name="row_forward",
    )(grid, gain, bias, table)
    return out.reshape(channels // 4, rows // 2, 8, wide)


def mid_kernel(x_ref, filt_ref, forward_ref, inverse_ref, out_ref, x_both, mixed):
    size, wide = mixed.shape[0] // 2, mixed.shape[1]
    rows = x_ref[...].astype(jnp.float32).reshape(size, wide)
    x_both[:size] = rows.astype(jnp.bfloat16)
    x_both[size:] = swap_parts(rows).astype(jnp.bfloat16)
    lat_len = size // 4
    for chan in range(4):
        part = pl.ds(chan * lat_len, lat_len)
        spec = jnp.dot(forward_ref[part], x_both[...], preferred_element_type=jnp.float32)
        tiles = []
        for lane in range(0, wide, 2 * LANES):
            half = pl.ds(lane // 2, LANES)
            filt_re, filt_im = filt_ref[0, part, half], filt_ref[1, part, half]
            spec_re = spec[:, lane : lane + LANES]
            spec_im = spec[:, lane + LANES : lane + 2 * LANES]
            tiles.append(spec_re * filt_re - spec_im * filt_im)
            tiles.append(spec_re * filt_im + spec_im * filt_re)
        both = jnp.concatenate(tiles, axis=1)
        mixed[part] = both.astype(jnp.bfloat16)
        mixed[pl.ds(size + chan * lat_len, lat_len)] = swap_parts(both, -1).astype(jnp.bfloat16)
    back = jnp.dot(inverse_ref[...], mixed[...], preferred_element_type=jnp.float32)
    out_ref[...] = back.reshape(out_ref.shape).astype(jnp.bfloat16)


def mid(slab, filt, forward, inverse, samples):
    devices, pairs, eight, wide = slab.shape
    spaces = devices // samples
    size = spaces * pairs * eight
    block = pl.BlockSpec((spaces, pairs, eight, wide), lambda s: (s, 0, 0, 0))
    once = pl.Buffered(1)
    return pl.pallas_call(
        mid_kernel,
        grid=(samples,),
        in_specs=[
            block,
            pl.BlockSpec((2, size, wide // 2), lambda s: (0, 0, 0), pipeline_mode=once),
            pl.BlockSpec((size, 2 * size), lambda s: (0, 0), pipeline_mode=once),
            pl.BlockSpec((size, 2 * size), lambda s: (0, 0), pipeline_mode=once),
        ],
        out_specs=block,
        out_shape=jax.ShapeDtypeStruct(slab.shape, jnp.bfloat16),
        scratch_shapes=[
            pltpu.VMEM((2 * size, wide), jnp.bfloat16),
            pltpu.VMEM((2 * size, wide), jnp.bfloat16),
        ],
        compiler_params=pltpu.CompilerParams(vmem_limit_bytes=VMEM),
        cost_estimate=pl.CostEstimate(
            flops=samples * 8 * size * size * wide,
            bytes_accessed=4 * samples * size * wide + 4 * size * (wide + 2 * size),
            transcendentals=0,
        ),
        name="columns",
    )(slab, filt, forward, inverse)


def post_kernel(back_ref, x_ref, table_ref, out_ref):
    first = back_ref[:, 0, 0].astype(jnp.float32)
    second = back_ref[:, 1, 0].astype(jnp.float32)
    top = first_half(first.shape)
    rows = (
        jnp.where(top, first, pltpu.roll(second, 4, axis=1)),
        jnp.where(top, pltpu.roll(first, 4, axis=1), second),
    )
    for row in range(2):
        spec = rows[row].reshape(first.shape[0] * 8, first.shape[2]).astype(jnp.bfloat16)
        branch = lax.dot_general(
            table_ref[...], spec, (((1,), (1,)), ((), ())), preferred_element_type=jnp.float32
        )
        out_ref[row] = (x_ref[row].astype(jnp.float32) + branch).astype(jnp.bfloat16)


def post(back, grid, table):
    rows, lon_len, channels = grid.shape
    wide = table.shape[1]
    block = pl.BlockSpec((2, lon_len, channels), lambda i: (i, 0, 0))
    return pl.pallas_call(
        post_kernel,
        grid=(rows // 2,),
        in_specs=[
            pl.BlockSpec((channels // 8, 2, 1, 8, wide), lambda i: (0, 0, i, 0, 0)),
            block,
            pl.BlockSpec((lon_len, wide), lambda i: (0, 0)),
        ],
        out_specs=block,
        out_shape=jax.ShapeDtypeStruct(grid.shape, jnp.bfloat16),
        compiler_params=pltpu.CompilerParams(vmem_limit_bytes=VMEM),
        cost_estimate=pl.CostEstimate(
            flops=2 * rows * lon_len * channels * wide,
            bytes_accessed=2 * rows * channels * (2 * lon_len + wide),
            transcendentals=0,
        ),
        name="row_inverse",
    )(back.reshape(channels // 8, 2, rows // 2, 8, wide), grid, table)


def filter_chunk(filt, start, wide):
    freqs = filt.shape[-1] // 2
    stop = min(start + wide // 2, freqs)
    by_chan = filt.transpose(1, 0, 2).reshape(-1, 2 * freqs)
    parts = [by_chan[:, first + start : first + stop] for first in (0, freqs)]
    return jnp.pad(jnp.stack(parts), ((0, 0), (0, 0), (0, wide // 2 - (stop - start))))


def swap_devices(blocks):
    return lax.all_to_all(blocks, BOTH, split_axis=0, concat_axis=0, tiled=True)


def shards(samples, norm_gain, norm_bias, spectral_filter):
    grid = samples[0]
    rows, lon_len, channels = grid.shape
    dp_count = lax.axis_size("dp")
    lat_len = rows * lax.axis_size("space")
    pieces = chunks(lon_len // 2 + 1)
    tables = [row_tables(lon_len, *piece) for piece in pieces]
    forward, inverse = column_tables(lat_len, spectral_filter.shape[1])
    gain, bias = norm_gain[None], norm_bias[None]
    slabs = [swap_devices(pre(grid, gain, bias, jnp.asarray(table[0]))) for table in tables]
    backs = [
        swap_devices(
            mid(
                slab,
                filter_chunk(spectral_filter, *piece),
                jnp.asarray(forward),
                jnp.asarray(inverse),
                dp_count,
            )
        )
        for slab, piece in zip(slabs, pieces)
    ]
    for back, table in zip(backs, tables):
        grid = post(back, grid, jnp.asarray(table[1]))
    return grid[None]


def solution(mesh):
    placed = (P("dp", "space", None, None), P(), P(), P(None, BOTH, None))
    return jax.shard_map(
        shards, mesh=mesh, in_specs=placed, out_specs=P("dp", "space", None, None), check_vma=False
    )
```

time: 257 us -> 261 us (1.016)
  waiting for transfers between devices: 78.5 us -> 107 us
  local copies, waits for them, and re-layouts: 24.4 us -> 9 us
  Pallas kernels: 108 us -> 101 us
  other arithmetic: 8.14 us -> 2.86 us
  starting transfers between devices: 34.1 us -> 38.1 us
    all_to_all x4, waiting for transfers between devices: 78.5 us -> 107 us  [swap_devices(): return lax.all_to_all(blocks, BOTH, split_axis=0, concat_axis=0, tiled=True)]
    unnamed x32 -> x0, local copies, waits for them, and re-layouts: 15.9 us -> none
    pallas_call x2, Pallas kernels: 70.1 us -> 55.6 us  [mid(): pl.pallas_call(mid_kernel, grid=(samples,), in_specs=[block, pl.BlockSpec...]
    pallas_call x2, Pallas kernels: 16.6 us -> 21.9 us  [post(): pl.pallas_call(post_kernel, grid=(rows // 2,), in_specs=[pl.BlockSpec((ch...]
    another operation x0 -> x2, local copies, waits for them, and re-layouts: none -> 4.16 us  [filter_chunk(): jnp.stack(parts)]
    all_to_all x4, starting transfers between devices: 34.1 us -> 38.1 us  [swap_devices(): return lax.all_to_all(blocks, BOTH, split_axis=0, concat_axis=0, tiled=True)]
    slice x5 -> x0, local copies, waits for them, and re-layouts: 3.54 us -> none  [the longest x1 2.65 us: lanes(): taken = by_chan[:, first + start:first + stop]]
    another operation x5 -> x2, other arithmetic: 5.44 us -> 2.86 us  [filter_chunk(): jnp.stack(parts)]
  transfers between devices with their start and end apart: 4 -> 4, of which waited for: 4 -> 3; matrix products, arithmetic and copies ran while one was open for 7% -> 5% of each run, Pallas kernels for 35% -> 30%
where the time goes in v2:
time: 261 us; the launch traced here: 258 us
  waiting for transfers between devices  107 us (41%)
  Pallas kernels  101 us (39%)
  starting transfers between devices  38.1 us (15%)
  local copies, waits for them, and re-layouts  9 us (3%)
  other arithmetic  2.86 us (1%)
    all_to_all x4, waiting for transfers between devices, swap_devices(): return lax.all_to_all(blocks, BOTH, split_axis=0, concat_axis=0, tiled=True)  107 us
    pallas_call x2, Pallas kernels, mid(): pl.pallas_call(mid_kernel, grid=(samples,), in_specs=[block, pl.BlockSpec...  55.6 us
    all_to_all x4, starting transfers between devices, swap_devices(): return lax.all_to_all(blocks, BOTH, split_axis=0, concat_axis=0, tiled=True)  38.1 us
    pallas_call x2, Pallas kernels, pre(): pl.pallas_call(pre_kernel, grid=(rows // 2,), in_specs=[pl.BlockSpec((2,...  23.2 us
    pallas_call x2, Pallas kernels, post(): pl.pallas_call(post_kernel, grid=(rows // 2,), in_specs=[pl.BlockSpec((ch...  21.9 us
  transfers between devices with their start and end apart: 4, of which 3 were waited for; matrix products, arithmetic and copies ran while one was open for 5% of the time, Pallas kernels for 30%

profile of v2, /device:TPU:14, one launch (start us, length us, event | category | flops | bytes accessed | tf_op | source)
XLA Modules:
  0.0 257.9 jit_solution(15972504833867665144)
XLA Ops:
  0.0 13.1 %row_forward.3 = bf16[64,2,5,8,512]{4,3,2,1,0:T(8,128)(2,1)} custom-call(bf16[10,720,512]{2,1,0:T(8,128)(2,1)} %bitcast.18, f32[1,512]{1,0:T(1,128)} %bitcast.25, f32[1,512]{1,0:T(1,128)} %bitcast.27, bf16[720,512]{1,0:T(8,128)(2,1)} %constant.15.clone.table_ref), custom_call_target="tpu_custom_call" | custom-call | flops 3774873600 | bytes 12615680 | tf_op jit(solution)/shard_map/row_forward/pallas_call | solution.py:97
  13.1 10.8 %all-to-all-start.2 = ((bf16[128,5,8,512]{3,2,1,0:T(8,128)(2,1)}), bf16[128,5,8,512]{3,2,1,0:T(8,128)(2,1)}, u32[]{:S(2)}, u32[]{:S(2)}) async-start(bf16[128,5,8,512]{3,2,1,0:T(8,128)(2,1)} %bitcast.23), calls=%async_computation.2 | async-start | bytes 10485760 | tf_op jit(solution)/shard_map/all_to_all | solution.py:223
  23.8 4.8 %copy.11 = f32[4,320,722]{2,1,0:T(8,128)} copy(f32[4,320,722]{2,0,1:T(4,128)} %bitcast.24) | data formatting | bytes 7393280 | tf_op jit(solution)/shard_map/transpose | solution.py:217
  28.7 10.1 %row_forward.2 = bf16[64,2,5,8,256]{4,3,2,1,0:T(8,128)(2,1)} custom-call(bf16[10,720,512]{2,1,0:T(8,128)(2,1)} %bitcast.19, f32[1,512]{1,0:T(1,128)} %bitcast.26, f32[1,512]{1,0:T(1,128)} %bitcast.28, bf16[720,256]{1,0:T(8,128)(2,1)} %constant.16.clone.table_ref), custom_call_target="tpu_custom_call" | custom-call | flops 1887436800 | bytes 9994240 | tf_op jit(solution)/shard_map/row_forward/pallas_call | solution.py:97
  38.8 2.4 slice_bitcast_fusion.1
  41.2 45.9 %all-to-all-done.2.x_ref = bf16[128,5,8,512]{3,2,1,0:T(8,128)(2,1)} async-done(((bf16[128,5,8,512]{3,2,1,0:T(8,128)(2,1)}), bf16[128,5,8,512]{3,2,1,0:T(8,128)(2,1)}, u32[]{:S(2)}, u32[]{:S(2)}) %all-to-all-start.2) | async-done | bytes 5242912 | tf_op jit(solution)/shard_map/all_to_all | solution.py:223
  87.1 8.6 %all-to-all-start = ((bf16[128,5,8,256]{3,2,1,0:T(8,128)(2,1)}), bf16[128,5,8,256]{3,2,1,0:T(8,128)(2,1)}, u32[]{:S(2)}, u32[]{:S(2)}) async-start(bf16[128,5,8,256]{3,2,1,0:T(8,128)(2,1)} %bitcast.3), calls=%async_computation | async-start | bytes 5242880 | tf_op jit(solution)/shard_map/all_to_all | solution.py:223
  95.7 1.6 pad_maximum_fusion.filt_ref
  97.4 35.1 %columns.3 = bf16[128,5,8,512]{3,2,1,0:T(8,128)(2,1)} custom-call(bf16[128,5,8,512]{3,2,1,0:T(8,128)(2,1)} %all-to-all-done.2.x_ref, f32[2,1280,256]{2,1,0:T(8,128)} %pad_maximum_fusion.filt_ref, bf16[1280,2560]{1,0:T(8,128)(2,1)} %constant.17.clone.forward_ref, bf16[1280,2560]{1,0:T(8,128)(2,1)} %constant.18.clone.inverse_ref), custom_call_target="tpu_custom_call" | custom-call | flops 26843545600 | bytes 26214400 | tf_op jit(solution)/shard_map/columns/pallas_call | solution.py:149
  132.5 0.0 all-to-all-done.x_ref
  132.5 10.2 %all-to-all-start.3 = ((bf16[128,5,8,512]{3,2,1,0:T(8,128)(2,1)}), bf16[128,5,8,512]{3,2,1,0:T(8,128)(2,1)}, u32[]{:S(2)}, u32[]{:S(2)}) async-start(bf16[128,5,8,512]{3,2,1,0:T(8,128)(2,1)} %columns.3), calls=%async_computation.3 | async-start | bytes 10485760 | tf_op jit(solution)/shard_map/all_to_all | solution.py:223
  142.7 1.8 slice_bitcast_fusion.3
  144.4 1.2 select_maximum_fusion.filt_ref
  145.7 20.5 %columns.2 = bf16[128,5,8,256]{3,2,1,0:T(8,128)(2,1)} custom-call(bf16[128,5,8,256]{3,2,1,0:T(8,128)(2,1)} %all-to-all-done.x_ref, f32[2,1280,128]{2,1,0:T(8,128)} %select_maximum_fusion.filt_ref, bf16[1280,2560]{1,0:T(8,128)(2,1)} %constant.17.clone.forward_ref, bf16[1280,2560]{1,0:T(8,128)(2,1)} %constant.18.clone.inverse_ref), custom_call_target="tpu_custom_call" | custom-call | flops 13421772800 | bytes 19660800 | tf_op jit(solution)/shard_map/columns/pallas_call | solution.py:149
  166.1 39.8 %all-to-all-done.3 = bf16[128,5,8,512]{3,2,1,0:T(8,128)(2,1)} async-done(((bf16[128,5,8,512]{3,2,1,0:T(8,128)(2,1)}), bf16[128,5,8,512]{3,2,1,0:T(8,128)(2,1)}, u32[]{:S(2)}, u32[]{:S(2)}) %all-to-all-start.3) | async-done | bytes 5242912 | tf_op jit(solution)/shard_map/all_to_all | solution.py:223
  205.9 8.5 %all-to-all-start.1 = ((bf16[128,5,8,256]{3,2,1,0:T(8,128)(2,1)}), bf16[128,5,8,256]{3,2,1,0:T(8,128)(2,1)}, u32[]{:S(2)}, u32[]{:S(2)}) async-start(bf16[128,5,8,256]{3,2,1,0:T(8,128)(2,1)} %columns.2), calls=%async_computation.1 | async-start | bytes 5242880 | tf_op jit(solution)/shard_map/all_to_all | solution.py:223
  214.5 12.0 %row_inverse.2.x_ref = bf16[10,720,512]{2,1,0:T(8,128)(2,1)} custom-call(bf16[64,2,5,8,512]{4,3,2,1,0:T(8,128)(2,1)} %bitcast.12.back_ref, bf16[10,720,512]{2,1,0:T(8,128)(2,1)} %bitcast.20, bf16[720,512]{1,0:T(8,128)(2,1)} %constant.19.clone.table_ref), custom_call_target="tpu_custom_call" | custom-call | flops 3774873600 | bytes 19988480 | tf_op jit(solution)/shard_map/row_inverse/pallas_call | solution.py:194
  226.4 21.4 %all-to-all-done.1 = bf16[128,5,8,256]{3,2,1,0:T(8,128)(2,1)} async-done(((bf16[128,5,8,256]{3,2,1,0:T(8,128)(2,1)}), bf16[128,5,8,256]{3,2,1,0:T(8,128)(2,1)}, u32[]{:S(2)}, u32[]{:S(2)}) %all-to-all-start.1) | async-done | bytes 2621472 | tf_op jit(solution)/shard_map/all_to_all | solution.py:223
  247.9 10.0 %row_inverse.3 = bf16[10,720,512]{2,1,0:T(8,128)(2,1)} custom-call(bf16[64,2,5,8,256]{4,3,2,1,0:T(8,128)(2,1)} %bitcast.8.back_ref, bf16[10,720,512]{2,1,0:T(8,128)(2,1)} %row_inverse.2.x_ref, bf16[720,256]{1,0:T(8,128)(2,1)} %constant.20.clone.table_ref), custom_call_target="tpu_custom_call" | custom-call | flops 1887436800 | bytes 17367040 | tf_op jit(solution)/shard_map/row_inverse/pallas_call | solution.py:194
Async XLA Ops:
  13.1 74.0 %all-to-all-start.2 = ((bf16[128,5,8,512]{3,2,1,0:T(8,128)(2,1)}), bf16[128,5,8,512]{3,2,1,0:T(8,128)(2,1)}, u32[]{:S(2)}, u32[]{:S(2)}) async-start(bf16[128,5,8,512]{3,2,1,0:T(8,128)(2,1)} %bitcast.23), calls=%async_computation.2 | async-start | bytes 10485760 | tf_op jit(solution)/shard_map/all_to_all | solution.py:223
  87.1 45.4 %all-to-all-start = ((bf16[128,5,8,256]{3,2,1,0:T(8,128)(2,1)}), bf16[128,5,8,256]{3,2,1,0:T(8,128)(2,1)}, u32[]{:S(2)}, u32[]{:S(2)}) async-start(bf16[128,5,8,256]{3,2,1,0:T(8,128)(2,1)} %bitcast.3), calls=%async_computation | async-start | bytes 5242880 | tf_op jit(solution)/shard_map/all_to_all | solution.py:223
  132.5 73.5 %all-to-all-start.3 = ((bf16[128,5,8,512]{3,2,1,0:T(8,128)(2,1)}), bf16[128,5,8,512]{3,2,1,0:T(8,128)(2,1)}, u32[]{:S(2)}, u32[]{:S(2)}) async-start(bf16[128,5,8,512]{3,2,1,0:T(8,128)(2,1)} %columns.3), calls=%async_computation.3 | async-start | bytes 10485760 | tf_op jit(solution)/shard_map/all_to_all | solution.py:223
  205.9 41.9 %all-to-all-start.1 = ((bf16[128,5,8,256]{3,2,1,0:T(8,128)(2,1)}), bf16[128,5,8,256]{3,2,1,0:T(8,128)(2,1)}, u32[]{:S(2)}, u32[]{:S(2)}) async-start(bf16[128,5,8,256]{3,2,1,0:T(8,128)(2,1)} %columns.2), calls=%async_computation.1 | async-start | bytes 5242880 | tf_op jit(solution)/shard_map/all_to_all | solution.py:223

commit v3 on v1

v3 whole, which is shorter than its diff:
```python
import functools
import math

import jax
import jax.numpy as jnp
import ml_dtypes
import numpy as np
from jax import lax
from jax.experimental import pallas as pl
from jax.experimental.pallas import tpu as pltpu
from jax.sharding import PartitionSpec as P

BOTH = ("dp", "space")
LANES = 128
WIDE = 3 * LANES
HALF = WIDE // 2
SPARE = 41
GUEST = 21
PAIRS = 5
MIB = 1024 * 1024
VMEM = 62 * MIB
ANY = pl.BlockSpec(memory_space=pl.ANY)


def lane_layout(start, freqs):
    lane = np.arange(WIDE)
    tail = lane >= 256
    imag = np.where(tail, lane >= 320, lane >= 128)
    freq = start + np.where(tail, 128 + lane % 64, lane % 128)
    return np.minimum(freq, freqs - 1), imag, freq < freqs


def row_tables(lon_len, start):
    freqs = lon_len // 2 + 1
    freq, imag, used = lane_layout(start, freqs)
    lon = np.arange(lon_len)
    turns = (lon[:, None] * freq[None, :] % lon_len).astype(np.float32) * np.float32(
        2.0 * math.pi / lon_len
    )
    scale = np.float32(1.0 / math.sqrt(lon_len))
    wave = np.where(imag, -np.sin(turns), np.cos(turns)) * used
    weight = np.where((freq == 0) | (freq == lon_len // 2), 1.0, 2.0).astype(np.float32)
    forward = (wave * scale).astype(ml_dtypes.bfloat16)
    inverse = (wave * weight * scale).astype(ml_dtypes.bfloat16)
    return forward.T, inverse


def guest_home(part):
    return part // 2 * 64 + part % 2 * GUEST


def guest_columns(table):
    guests = np.zeros((table.shape[0], 4 * LANES), table.dtype)
    for part in range(4):
        home = 2 * LANES + guest_home(part)
        width = min(GUEST, SPARE - part % 2 * GUEST)
        seat = part * LANES + SPARE
        guests[:, seat : seat + width] = table[:, home : home + width]
    return np.concatenate([table[:, : 2 * LANES], guests], axis=1)


def column_tables(spaces, rows, chan_part):
    lat_len = spaces * rows
    lat = np.arange(lat_len)
    turns = (lat[:, None] * lat[None, :] % lat_len).astype(np.float32) * np.float32(
        2.0 * math.pi / lat_len
    )
    scale = np.float32(1.0 / math.sqrt(lat_len))
    size = chan_part * lat_len
    order = lat.reshape(spaces, rows // 2, 2).transpose(1, 0, 2).reshape(-1)
    forward = np.zeros((chan_part, lat_len, 2, lat_len, chan_part), np.float32)
    for chan in range(chan_part):
        forward[chan, :, 0, :, chan] = (np.cos(turns) * scale)[:, order]
        forward[chan, :, 1, :, chan] = (np.sin(turns) * scale)[:, order]
    inverse = forward.transpose(3, 4, 2, 0, 1).reshape(size, 2 * size)
    forward = forward.reshape(size, 2 * size)
    return forward.astype(ml_dtypes.bfloat16), inverse.astype(ml_dtypes.bfloat16)


def swap_parts(values):
    tail = values[:, 2 * LANES :]
    return jnp.concatenate(
        [values[:, LANES : 2 * LANES], values[:, :LANES], pltpu.roll(tail, 64, axis=1)], axis=1
    )


def imag_lanes(shape):
    lane = lax.broadcasted_iota(jnp.int32, shape, len(shape) - 1)
    return ((lane >= LANES) & (lane < 2 * LANES)) | (lane >= 320)


def first_half(shape):
    return lax.broadcasted_iota(jnp.int32, shape, 1) < 4


def interleave(one, two):
    top = first_half(one.shape)
    return (
        jnp.where(top, one, pltpu.roll(two, 4, axis=1)),
        jnp.where(top, pltpu.roll(one, 4, axis=1), two),
    )


def normed_row(values, gain, bias):
    wide = values.astype(jnp.float32)
    center = jnp.mean(wide, axis=-1, keepdims=True)
    wide = wide - center
    spread = jnp.mean(jnp.square(wide), axis=-1, keepdims=True)
    return (wide * lax.rsqrt(spread + 1e-05) * gain + bias).astype(jnp.bfloat16)


def pair_spectra(x_ref, gain_ref, bias_ref, table):
    specs = []
    for row in range(2):
        normed = normed_row(x_ref[row], gain_ref[...], bias_ref[...])
        spec = jnp.dot(table, normed, preferred_element_type=jnp.float32).T
        specs.append(spec.reshape(spec.shape[0] // 8, 8, spec.shape[1]))
    return interleave(*specs)


def pre_kernel(x_ref, gain_ref, bias_ref, table_ref, out_ref):
    both = pair_spectra(x_ref, gain_ref, bias_ref, table_ref[...])
    for side in range(2):
        out_ref[:, side, 0] = both[side].astype(jnp.bfloat16)


def pre_packed_kernel(x_ref, gain_ref, bias_ref, table_ref, last_ref, out_ref):
    pair = pl.program_id(0)

    def main(both):
        for side in range(2):
            for tile in range(2):
                out_ref[:, side, 2 * pair + tile] = both[side][
                    :, :, tile * LANES : (tile + 1) * LANES
                ].astype(jnp.bfloat16)

    @pl.when(pair < PAIRS - 1)
    def _():
        both = pair_spectra(x_ref, gain_ref, bias_ref, table_ref[...])
        main(both)
        for side in range(2):
            out_ref[:, side, 2 * PAIRS + pair] = both[side][:, :, 2 * LANES :].astype(jnp.bfloat16)

    @pl.when(pair == PAIRS - 1)
    def _():
        both = pair_spectra(x_ref, gain_ref, bias_ref, last_ref[...])
        main(both)
        for side in range(2):
            for part in range(4):
                guest = both[side][:, :, (2 + part) * LANES : (3 + part) * LANES]
                tail = out_ref[:, side, 2 * PAIRS + part].astype(jnp.float32)
                out_ref[:, side, 2 * PAIRS + part] = (tail + guest).astype(jnp.bfloat16)


def pre(grid, gain, bias, table, packed):
    rows, lon_len, channels = grid.shape
    groups = channels // 8
    if packed:
        kernel = pre_packed_kernel
        shape = (groups, 2, 3 * PAIRS - 1, 8, LANES)
        out_spec = pl.BlockSpec(shape, lambda i: (0, 0, 0, 0, 0))
        tables = (table, guest_columns(table.T).T)
    else:
        kernel = pre_kernel
        shape = (groups, 2, PAIRS, 8, WIDE)
        out_spec = pl.BlockSpec((groups, 2, 1, 8, WIDE), lambda i: (0, 0, i, 0, 0))
        tables = (table,)
    out = pl.pallas_call(
        kernel,
        grid=(rows // 2,),
        in_specs=[
            pl.BlockSpec((2, lon_len, channels), lambda i: (i, 0, 0)),
            pl.BlockSpec((1, channels), lambda i: (0, 0)),
            pl.BlockSpec((1, channels), lambda i: (0, 0)),
        ]
        + [pl.BlockSpec(each.shape, lambda i: (0, 0)) for each in tables],
        out_specs=out_spec,
        out_shape=jax.ShapeDtypeStruct(shape, jnp.bfloat16),
        compiler_params=pltpu.CompilerParams(vmem_limit_bytes=VMEM),
        cost_estimate=pl.CostEstimate(
            flops=2 * rows * lon_len * channels * WIDE,
            bytes_accessed=2 * rows * channels * (lon_len + WIDE),
            transcendentals=rows * lon_len,
        ),
        name="row_forward",
    )(grid, gain, bias, *(jnp.asarray(each) for each in tables))
    return out.reshape(2 * groups, *shape[2:])


def guest_lanes(shape, first):
    lane = lax.broadcasted_iota(jnp.int32, shape, 1)
    return (lane >= first) & (lane < first + GUEST)


def load_pairs(x_ref, packed):
    pairs = []
    if not packed:
        for pair in range(PAIRS):
            rows = x_ref[:, pair].astype(jnp.float32)
            pairs.append(rows.reshape(rows.shape[0] * 8, WIDE))
        return pairs
    tiles = []
    for tile in range(3 * PAIRS - 1):
        rows = x_ref[:, tile].astype(jnp.float32)
        tiles.append(rows.reshape(rows.shape[0] * 8, LANES))
    tails = tiles[2 * PAIRS :]
    last = jnp.zeros_like(tails[0])
    for part in range(4):
        home = guest_home(part)
        moved = pltpu.roll(tails[part], (home - SPARE) % LANES, axis=1)
        last = jnp.where(guest_lanes(last.shape, home), moved, last)
    tails.append(last)
    for pair in range(PAIRS):
        pairs.append(jnp.concatenate([tiles[2 * pair], tiles[2 * pair + 1], tails[pair]], axis=1))
    return pairs


def store_pairs(out_ref, back, packed):
    count = back.shape[0] // PAIRS
    pairs = [back[pair * count : (pair + 1) * count] for pair in range(PAIRS)]
    if not packed:
        for pair in range(PAIRS):
            out_ref[:, pair] = pairs[pair].reshape(count // 8, 8, WIDE).astype(jnp.bfloat16)
        return
    tails = [rows[:, 2 * LANES :] for rows in pairs]
    for part in range(4):
        moved = pltpu.roll(tails[-1], (SPARE - guest_home(part)) % LANES, axis=1)
        tails[part] = jnp.where(guest_lanes(moved.shape, SPARE), moved, tails[part])
    tiles = []
    for rows in pairs:
        tiles += [rows[:, :LANES], rows[:, LANES : 2 * LANES]]
    for index, tile in enumerate(tiles + tails[:-1]):
        out_ref[:, index] = tile.reshape(count // 8, 8, LANES).astype(jnp.bfloat16)


def mid_kernel(packed, x_ref, filt_ref, forward_ref, inverse_ref, out_ref, x_both, mixed):
    size = x_both.shape[0] // 2
    count = size // PAIRS
    for pair, rows in enumerate(load_pairs(x_ref, packed)):
        turned = swap_parts(rows)
        x_both[pl.ds(pair * count, count)] = rows.astype(jnp.bfloat16)
        x_both[pl.ds(size + pair * count, count)] = jnp.where(
            imag_lanes(rows.shape), -turned, turned
        ).astype(jnp.bfloat16)
    lat_len = size // 4
    for chan in range(4):
        part = pl.ds(chan * lat_len, lat_len)
        spec = jnp.dot(forward_ref[part], x_both[...], preferred_element_type=jnp.float32)
        both = filt_ref[0, part] * spec + filt_ref[1, part] * swap_parts(spec)
        turned = swap_parts(both)
        mixed[part] = both.astype(jnp.bfloat16)
        mixed[pl.ds(size + chan * lat_len, lat_len)] = jnp.where(
            imag_lanes(both.shape), turned, -turned
        ).astype(jnp.bfloat16)
    back = jnp.dot(inverse_ref[...], mixed[...], preferred_element_type=jnp.float32)
    store_pairs(out_ref, back, packed)


def mid(slab, filt, forward, inverse, samples, packed):
    spaces = slab.shape[0] // samples
    size = forward.shape[0]
    block = pl.BlockSpec((spaces, *slab.shape[1:]), lambda s: (s, 0, 0, 0))
    once = pl.Buffered(1)
    return pl.pallas_call(
        functools.partial(mid_kernel, packed),
        grid=(samples,),
        in_specs=[
            block,
            pl.BlockSpec((2, size, WIDE), lambda s: (0, 0, 0), pipeline_mode=once),
            pl.BlockSpec((size, 2 * size), lambda s: (0, 0), pipeline_mode=once),
            pl.BlockSpec((size, 2 * size), lambda s: (0, 0), pipeline_mode=once),
        ],
        out_specs=block,
        out_shape=jax.ShapeDtypeStruct(slab.shape, jnp.bfloat16),
        scratch_shapes=[
            pltpu.VMEM((2 * size, WIDE), jnp.bfloat16),
            pltpu.VMEM((2 * size, WIDE), jnp.bfloat16),
        ],
        compiler_params=pltpu.CompilerParams(vmem_limit_bytes=VMEM),
        cost_estimate=pl.CostEstimate(
            flops=samples * 8 * size * size * WIDE,
            bytes_accessed=4 * samples * size * WIDE + 8 * size * (WIDE + size),
            transcendentals=0,
        ),
        name="columns",
    )(slab, filt, forward, inverse)


def post_kernel(packed, back_hbm, x_hbm, *refs):
    tables = refs[: 1 + packed]
    out_hbm, x_in, out, x_sem, out_sem = refs[1 + packed : 6 + packed]
    mains, main_sem, *tail_refs = refs[6 + packed :]

    def main_copy(pair):
        source = back_hbm.at[:, :, pl.ds(2 * pair, 2)] if packed else back_hbm.at[:, :, pair]
        return pltpu.make_async_copy(source, mains.at[pair], main_sem.at[pair])

    def tail_copy(pair):
        tails, tail_sem = tail_refs
        return pltpu.make_async_copy(
            back_hbm.at[:, :, 2 * PAIRS + pair], tails.at[pair], tail_sem.at[pair]
        )

    def x_copy(pair):
        return pltpu.make_async_copy(x_hbm.at[pl.ds(2 * pair, 2)], x_in.at[pair], x_sem.at[pair])

    def out_copy(pair):
        return pltpu.make_async_copy(out.at[pair], out_hbm.at[pl.ds(2 * pair, 2)], out_sem.at[pair])

    for pair in range(PAIRS):
        main_copy(pair).start()
        if packed and pair < PAIRS - 1:
            tail_copy(pair).start()
        x_copy(pair).start()
    for pair in range(PAIRS):
        main_copy(pair).wait()
        if packed and pair < PAIRS - 1:
            tail_copy(pair).wait()
        if packed:
            sides = [[mains[pair, :, side, tile] for side in range(2)] for tile in range(2)]
            for part in [pair] if pair < PAIRS - 1 else range(4):
                sides.append([tail_refs[0][part, :, side] for side in range(2)])
        else:
            sides = [[mains[pair, :, side] for side in range(2)]]
        tiles = [interleave(*(each.astype(jnp.float32) for each in both)) for both in sides]
        table = tables[packed and pair == PAIRS - 1]
        x_copy(pair).wait()
        for row in range(2):
            spec = [tile[row].reshape(tile[row].shape[0] * 8, -1) for tile in tiles]
            spec = jnp.concatenate([each.astype(jnp.bfloat16) for each in spec], axis=1)
            branch = lax.dot_general(
                table[...], spec, (((1,), (1,)), ((), ())), preferred_element_type=jnp.float32
            )
            out[pair, row] = (x_in[pair, row].astype(jnp.float32) + branch).astype(jnp.bfloat16)
        out_copy(pair).start()
    for pair in range(PAIRS):
        out_copy(pair).wait()


def post(back, grid, table, packed):
    rows, lon_len, channels = grid.shape
    groups = channels // 8
    tables = (table, guest_columns(table)) if packed else (table,)
    main = (PAIRS, groups, 2, 2, 8, LANES) if packed else (PAIRS, groups, 2, 8, WIDE)
    scratch = [
        pltpu.VMEM((PAIRS, 2, lon_len, channels), jnp.bfloat16),
        pltpu.VMEM((PAIRS, 2, lon_len, channels), jnp.bfloat16),
        pltpu.SemaphoreType.DMA((PAIRS,)),
        pltpu.SemaphoreType.DMA((PAIRS,)),
        pltpu.VMEM(main, jnp.bfloat16),
        pltpu.SemaphoreType.DMA((PAIRS,)),
    ]
    if packed:
        scratch += [
            pltpu.VMEM((PAIRS - 1, groups, 2, 8, LANES), jnp.bfloat16),
            pltpu.SemaphoreType.DMA((PAIRS - 1,)),
        ]
    return pl.pallas_call(
        functools.partial(post_kernel, packed),
        in_specs=[ANY, ANY] + [pl.BlockSpec(memory_space=pltpu.VMEM)] * len(tables),
        out_specs=ANY,
        out_shape=jax.ShapeDtypeStruct(grid.shape, jnp.bfloat16),
        scratch_shapes=scratch,
        compiler_params=pltpu.CompilerParams(vmem_limit_bytes=VMEM),
        cost_estimate=pl.CostEstimate(
            flops=2 * rows * lon_len * channels * WIDE,
            bytes_accessed=2 * rows * channels * (2 * lon_len + WIDE),
            transcendentals=0,
        ),
        name="row_inverse",
    )(
        back.reshape(groups, 2, *back.shape[1:]),
        grid,
        *(jnp.asarray(each) for each in tables),
    )


def filter_chunk(filt, start):
    freqs = filt.shape[-1] // 2
    by_chan = filt.transpose(1, 0, 2).reshape(-1, 2 * freqs)

    def lanes(first):
        stop = min(start + HALF, freqs)
        taken = by_chan[:, first + start : first + stop]
        return jnp.pad(taken, ((0, 0), (0, HALF - taken.shape[1])))

    real, imag = lanes(0), lanes(freqs)

    def lay(one, two):
        return jnp.concatenate(
            [one[:, :LANES], two[:, :LANES], one[:, LANES:], two[:, LANES:]], axis=1
        )

    return jnp.stack([lay(real, real), lay(-imag, imag)])


def swap_devices(blocks):
    return lax.all_to_all(blocks, BOTH, split_axis=0, concat_axis=0, tiled=True)


def shards(samples, norm_gain, norm_bias, spectral_filter):
    grid = samples[0]
    rows, lon_len, _ = grid.shape
    dp_count = lax.axis_size("dp")
    starts = (0, HALF)
    tables = [row_tables(lon_len, start) for start in starts]
    columns = column_tables(lax.axis_size("space"), rows, spectral_filter.shape[1])
    forward, inverse = (jnp.asarray(each) for each in columns)
    gain, bias = norm_gain[None], norm_bias[None]
    slabs = [
        swap_devices(pre(grid, gain, bias, tables[index][0], index == 1)) for index in range(2)
    ]
    backs = []
    for index in range(2):
        filt = filter_chunk(spectral_filter, starts[index])
        back = mid(slabs[index], filt, forward, inverse, dp_count, index == 1)
        backs.append(swap_devices(back))
    for index in range(2):
        grid = post(backs[index], grid, tables[index][1], index == 1)
    return grid[None]


def solution(mesh):
    placed = (P("dp", "space", None, None), P(), P(), P(None, BOTH, None))
    return jax.shard_map(
        shards, mesh=mesh, in_specs=placed, out_specs=P("dp", "space", None, None), check_vma=False
    )
```

time: 257 us -> 245 us (0.953)
  local copies, waits for them, and re-layouts: 24.4 us -> 14.8 us
  waiting for transfers between devices: 78.5 us -> 69.8 us
  Pallas kernels: 108 us -> 115 us
    unnamed x32 -> x8, local copies, waits for them, and re-layouts: 15.9 us -> 2.42 us
    all_to_all x4, waiting for transfers between devices: 78.5 us -> 69.8 us  [swap_devices(): return lax.all_to_all(blocks, BOTH, split_axis=0, concat_axis=0, tiled=True)]
    pallas_call x6, Pallas kernels: 108 us -> 115 us  [the longest x2 70.4 us: mid(): pl.pallas_call(functools.partial(mid_kernel, packed), grid=(samples,), in...]
    slice x4, local copies, waits for them, and re-layouts: 0.9 us -> 6.81 us  [the longest x2 5 us: lay(): one[:, :LANES]]
  transfers between devices with their start and end apart: 4 -> 4, of which waited for: 4 -> 4; matrix products, arithmetic and copies ran while one was open for 7% -> 8% of each run, Pallas kernels for 35% -> 39%
where the time goes in v3:
time: 245 us; the launch traced here: 242 us
  Pallas kernels  115 us (47%)
  waiting for transfers between devices  69.8 us (28%)
  starting transfers between devices  35.6 us (15%)
  local copies, waits for them, and re-layouts  14.8 us (6%)
  other arithmetic  6.06 us (2%)
    pallas_call x2, Pallas kernels, mid(): pl.pallas_call(functools.partial(mid_kernel, packed), grid=(samples,), in...  70.4 us
    all_to_all x4, waiting for transfers between devices, swap_devices(): return lax.all_to_all(blocks, BOTH, split_axis=0, concat_axis=0, tiled=True)  69.8 us
    all_to_all x4, starting transfers between devices, swap_devices(): return lax.all_to_all(blocks, BOTH, split_axis=0, concat_axis=0, tiled=True)  35.6 us
    pallas_call x2, Pallas kernels, pre(): pl.pallas_call(kernel, grid=(rows // 2,), in_specs=[pl.BlockSpec((2, lon_...  23.7 us
    pallas_call x2, Pallas kernels, post(): pl.pallas_call(functools.partial(post_kernel, packed), in_specs=[ANY, ANY...  20.8 us
    another operation x5, other arithmetic, filter_chunk(): return jnp.stack([lay(real, real), lay(-imag, imag)])  5.46 us
    slice x2, local copies, waits for them, and re-layouts, lay(): one[:, :LANES]  5 us
  transfers between devices with their start and end apart: 4, of which 4 were waited for; matrix products, arithmetic and copies ran while one was open for 8% of the time, Pallas kernels for 39%

profile of v3, /device:TPU:14, one launch (start us, length us, event | category | flops | bytes accessed | tf_op | source)
XLA Modules:
  0.0 241.6 jit_solution(5195407583619467344)
XLA Ops:
  0.0 11.0 %row_forward.3 = bf16[64,2,5,8,384]{4,3,2,1,0:T(8,128)(2,1)} custom-call(bf16[10,720,512]{2,1,0:T(8,128)(2,1)} %bitcast.18, f32[1,512]{1,0:T(1,128)} %bitcast.28, f32[1,512]{1,0:T(1,128)} %bitcast.30, bf16[384,720]{1,0:T(8,128)(2,1)} %constant.21.clone.table_ref), custom_call_target="tpu_custom_call" | custom-call | flops 2831155200 | bytes 11304960 | tf_op jit(solution)/shard_map/row_forward/pallas_call | solution.py:168
  11.0 10.8 %all-to-all-start.2 = ((bf16[128,5,8,384]{3,2,1,0:T(8,128)(2,1)}), bf16[128,5,8,384]{3,2,1,0:T(8,128)(2,1)}, u32[]{:S(2)}, u32[]{:S(2)}) async-start(bf16[128,5,8,384]{3,2,1,0:T(8,128)(2,1)} %bitcast.25), calls=%async_computation.2 | async-start | bytes 7864320 | tf_op jit(solution)/shard_map/all_to_all | solution.py:398
  21.7 2.9 %copy.13 = f32[4,320,722]{2,1,0:T(8,128)S(1)} copy(f32[4,320,722]{2,0,1:T(4,128)} %bitcast.27) | data formatting | bytes 7393280 | tf_op jit(solution)/shard_map/transpose | solution.py:380
  25.1 1.5 copy-done
  26.6 1.0 slice.86
  27.5 12.8 %row_forward.2 = bf16[64,2,14,8,128]{4,3,2,1,0:T(8,128)(2,1)} custom-call(bf16[10,720,512]{2,1,0:T(8,128)(2,1)} %bitcast.19, f32[1,512]{1,0:T(1,128)} %bitcast.29, f32[1,512]{1,0:T(1,128)} %bitcast.31, bf16[384,720]{1,0:T(8,128)(2,1)} %constant.22.clone.table_ref, bf16[768,720]{1,0:T(8,128)(2,1)} %constant.23.clone.last_ref), custom_call_target="tpu_custom_call" | custom-call | flops 2831155200 | bytes 11304960 | tf_op jit(solution)/shard_map/row_forward/pallas_call | solution.py:168
  40.3 28.9 %all-to-all-done.2.x_ref = bf16[128,5,8,384]{3,2,1,0:T(8,128)(2,1)} async-done(((bf16[128,5,8,384]{3,2,1,0:T(8,128)(2,1)}), bf16[128,5,8,384]{3,2,1,0:T(8,128)(2,1)}, u32[]{:S(2)}, u32[]{:S(2)}) %all-to-all-start.2) | async-done | bytes 3932192 | tf_op jit(solution)/shard_map/all_to_all | solution.py:398
  69.2 7.8 %all-to-all-start = ((bf16[128,14,8,128]{3,2,1,0:T(8,128)(2,1)}), bf16[128,14,8,128]{3,2,1,0:T(8,128)(2,1)}, u32[]{:S(2)}, u32[]{:S(2)}) async-start(bf16[128,14,8,128]{3,2,1,0:T(8,128)(2,1)} %bitcast.26), calls=%async_computation | async-start | bytes 7340032 | tf_op jit(solution)/shard_map/all_to_all | solution.py:398
  77.0 1.8 fusion.3
  78.7 4.0 %fusion.1 = (f32[1280,128]{1,0:T(8,128)S(1)}, f32[1280,128]{1,0:T(8,128)S(1)}, f32[1280,128]{1,0:T(8,128)}, f32[1280,128]{1,0:T(8,128)}) fusion(f32[1280,722]{1,0:T(8,128)} %bitcast.23), kind=kLoop, calls=%fused_computation.12 | loop fusion | bytes 5242880 | tf_op jit(solution)/shard_map/slice | solution.py:391
  82.8 0.5 maximum_bitcast_fusion.2
  83.3 2.2 pad_maximum_fusion.1.filt_ref
  85.5 35.1 %columns.3 = bf16[128,5,8,384]{3,2,1,0:T(8,128)(2,1)} custom-call(bf16[128,5,8,384]{3,2,1,0:T(8,128)(2,1)} %all-to-all-done.2.x_ref, f32[2,1280,384]{2,1,0:T(8,128)} %pad_maximum_fusion.1.filt_ref, bf16[1280,2560]{1,0:T(8,128)(2,1)} %constant.19.clone.forward_ref, bf16[1280,2560]{1,0:T(8,128)(2,1)} %constant.20.clone.inverse_ref), custom_call_target="tpu_custom_call" | custom-call | flops 20132659200 | bytes 24903680 | tf_op jit(solution)/shard_map/columns/pallas_call | solution.py:264
  120.6 0.9 all-to-all-done.x_ref
  121.5 9.3 %all-to-all-start.3 = ((bf16[128,5,8,384]{3,2,1,0:T(8,128)(2,1)}), bf16[128,5,8,384]{3,2,1,0:T(8,128)(2,1)}, u32[]{:S(2)}, u32[]{:S(2)}) async-start(bf16[128,5,8,384]{3,2,1,0:T(8,128)(2,1)} %columns.3), calls=%async_computation.3 | async-start | bytes 7864320 | tf_op jit(solution)/shard_map/all_to_all | solution.py:398
  130.8 2.6 %fusion.4 = (f32[1280,169]{1,0:T(8,128)S(1)}, f32[1280,169]{1,0:T(8,128)S(1)}) fusion(f32[1280,722]{1,0:T(8,128)} %bitcast.24), kind=kLoop, calls=%fused_computation.15 | loop fusion | bytes 3461120 | tf_op jit(solution)/shard_map/slice | solution.py:384
  133.6 0.9 copy-done.3
  135.1 2.2 pad_maximum_fusion.filt_ref
  137.3 35.4 %columns.2 = bf16[128,14,8,128]{3,2,1,0:T(8,128)(2,1)} custom-call(bf16[128,14,8,128]{3,2,1,0:T(8,128)(2,1)} %all-to-all-done.x_ref, f32[2,1280,384]{2,1,0:T(8,128)} %pad_maximum_fusion.filt_ref, bf16[1280,2560]{1,0:T(8,128)(2,1)} %constant.19.clone.forward_ref, bf16[1280,2560]{1,0:T(8,128)(2,1)} %constant.20.clone.inverse_ref), custom_call_target="tpu_custom_call" | custom-call | flops 20132659200 | bytes 24903680 | tf_op jit(solution)/shard_map/columns/pallas_call | solution.py:264
  172.7 5.5 %all-to-all-done.3 = bf16[128,5,8,384]{3,2,1,0:T(8,128)(2,1)} async-done(((bf16[128,5,8,384]{3,2,1,0:T(8,128)(2,1)}), bf16[128,5,8,384]{3,2,1,0:T(8,128)(2,1)}, u32[]{:S(2)}, u32[]{:S(2)}) %all-to-all-start.3) | async-done | bytes 3932192 | tf_op jit(solution)/shard_map/all_to_all | solution.py:398
  178.2 7.8 %all-to-all-start.1 = ((bf16[128,14,8,128]{3,2,1,0:T(8,128)(2,1)}), bf16[128,14,8,128]{3,2,1,0:T(8,128)(2,1)}, u32[]{:S(2)}, u32[]{:S(2)}) async-start(bf16[128,14,8,128]{3,2,1,0:T(8,128)(2,1)} %columns.2), calls=%async_computation.1 | async-start | bytes 7340032 | tf_op jit(solution)/shard_map/all_to_all | solution.py:398
  186.0 9.9 %row_inverse.2.x_hbm = bf16[10,720,512]{2,1,0:T(8,128)(2,1)} custom-call(bf16[64,2,5,8,384]{4,3,2,1,0:T(8,128)(2,1)} %bitcast.12.back_hbm, bf16[10,720,512]{2,1,0:T(8,128)(2,1)} %bitcast.20, bf16[720,384]{1,0:T(8,128)(2,1)} %constant.24.clone.refs_0_), custom_call_target="tpu_custom_call" | custom-call | flops 2831155200 | bytes 18677760 | tf_op jit(solution)/shard_map/row_inverse/pallas_call | solution.py:358
  195.9 34.6 %all-to-all-done.1 = bf16[128,14,8,128]{3,2,1,0:T(8,128)(2,1)} async-done(((bf16[128,14,8,128]{3,2,1,0:T(8,128)(2,1)}), bf16[128,14,8,128]{3,2,1,0:T(8,128)(2,1)}, u32[]{:S(2)}, u32[]{:S(2)}) %all-to-all-start.1) | async-done | bytes 3670048 | tf_op jit(solution)/shard_map/all_to_all | solution.py:398
  230.5 10.9 %row_inverse.3 = bf16[10,720,512]{2,1,0:T(8,128)(2,1)} custom-call(bf16[64,2,14,8,128]{4,3,2,1,0:T(8,128)(2,1)} %bitcast.8.back_hbm, bf16[10,720,512]{2,1,0:T(8,128)(2,1)} %row_inverse.2.x_hbm, bf16[720,384]{1,0:T(8,128)(2,1)} %constant.25.clone.refs_0_, bf16[720,768]{1,0:T(8,128)(2,1)} %constant.26.clone.refs_1_), custom_call_target="tpu_custom_call" | custom-call | flops 2831155200 | bytes 18677760 | tf_op jit(solution)/shard_map/row_inverse/pallas_call | solution.py:358
  (12 shorter events, 1.2 us)
Async XLA Ops:
  11.0 58.2 %all-to-all-start.2 = ((bf16[128,5,8,384]{3,2,1,0:T(8,128)(2,1)}), bf16[128,5,8,384]{3,2,1,0:T(8,128)(2,1)}, u32[]{:S(2)}, u32[]{:S(2)}) async-start(bf16[128,5,8,384]{3,2,1,0:T(8,128)(2,1)} %bitcast.25), calls=%async_computation.2 | async-start | bytes 7864320 | tf_op jit(solution)/shard_map/all_to_all | solution.py:398
  24.6 1.9 copy-start
  69.2 52.3 %all-to-all-start = ((bf16[128,14,8,128]{3,2,1,0:T(8,128)(2,1)}), bf16[128,14,8,128]{3,2,1,0:T(8,128)(2,1)}, u32[]{:S(2)}, u32[]{:S(2)}) async-start(bf16[128,14,8,128]{3,2,1,0:T(8,128)(2,1)} %bitcast.26), calls=%async_computation | async-start | bytes 7340032 | tf_op jit(solution)/shard_map/all_to_all | solution.py:398
  78.7 4.1 %copy-start.1 = (f32[1280,128]{1,0:T(8,128)S(1)}, f32[1280,128]{1,0:T(8,128)}, u32[]{:S(2)}) copy-start(f32[1280,128]{1,0:T(8,128)} %slice.86) | copy-start | bytes 1966084
  121.5 56.7 %all-to-all-start.3 = ((bf16[128,5,8,384]{3,2,1,0:T(8,128)(2,1)}), bf16[128,5,8,384]{3,2,1,0:T(8,128)(2,1)}, u32[]{:S(2)}, u32[]{:S(2)}) async-start(bf16[128,5,8,384]{3,2,1,0:T(8,128)(2,1)} %columns.3), calls=%async_computation.3 | async-start | bytes 7864320 | tf_op jit(solution)/shard_map/all_to_all | solution.py:398
  133.5 1.1 copy-start.3
  133.6 1.2 copy-start.2
  178.2 52.3 %all-to-all-start.1 = ((bf16[128,14,8,128]{3,2,1,0:T(8,128)(2,1)}), bf16[128,14,8,128]{3,2,1,0:T(8,128)(2,1)}, u32[]{:S(2)}, u32[]{:S(2)}) async-start(bf16[128,14,8,128]{3,2,1,0:T(8,128)(2,1)} %columns.2), calls=%async_computation.1 | async-start | bytes 7340032 | tf_op jit(solution)/shard_map/all_to_all | solution.py:398

commit v4 on v3

--- a/solution.py
+++ b/solution.py
@@ -361,7 +361,7 @@
         out_specs=ANY,
         out_shape=jax.ShapeDtypeStruct(grid.shape, jnp.bfloat16),
         scratch_shapes=scratch,
-        compiler_params=pltpu.CompilerParams(vmem_limit_bytes=VMEM),
+        compiler_params=pltpu.CompilerParams(vmem_limit_bytes=VMEM - MIB),
         cost_estimate=pl.CostEstimate(
             flops=2 * rows * lon_len * channels * WIDE,
             bytes_accessed=2 * rows * channels * (2 * lon_len + WIDE),
@@ -407,13 +407,13 @@
     columns = column_tables(lax.axis_size("space"), rows, spectral_filter.shape[1])
     forward, inverse = (jnp.asarray(each) for each in columns)
     gain, bias = norm_gain[None], norm_bias[None]
-    slabs = [
-        swap_devices(pre(grid, gain, bias, tables[index][0], index == 1)) for index in range(2)
-    ]
+    spectra = [pre(grid, gain, bias, tables[index][0], index == 1) for index in range(2)]
+    filts = [filter_chunk(spectral_filter, start) for start in starts]
+    spectra[1], filts = lax.optimization_barrier((spectra[1], filts))
+    slabs = [swap_devices(each) for each in spectra]
     backs = []
     for index in range(2):
-        filt = filter_chunk(spectral_filter, starts[index])
-        back = mid(slabs[index], filt, forward, inverse, dp_count, index == 1)
+        back = mid(slabs[index], filts[index], forward, inverse, dp_count, index == 1)
         backs.append(swap_devices(back))
     for index in range(2):
         grid = post(backs[index], grid, tables[index][1], index == 1)

time: 245 us -> 243 us (level)
  local copies, waits for them, and re-layouts: 14.8 us -> 10.1 us
  waiting for transfers between devices: 69.8 us -> 72.3 us
    slice x2, local copies, waits for them, and re-layouts: 5 us -> 1.47 us  [lay(): one[:, :LANES]]
    another operation x5 -> x4, other arithmetic: 5.46 us -> 5.4 us  [filter_chunk(): return jnp.stack([lay(real, real), lay(-imag, imag)])]
  transfers between devices with their start and end apart: 4 -> 4, of which waited for: 4 -> 4; matrix products, arithmetic and copies ran while one was open for 8% -> 7% of each run, Pallas kernels for 39% -> 39%
where the time goes in v4:
time: 243 us; the launch traced here: 240 us
  Pallas kernels  115 us (47%)
  waiting for transfers between devices  72.3 us (30%)
  starting transfers between devices  33.9 us (14%)
  local copies, waits for them, and re-layouts  10.1 us (4%)
  other arithmetic  8.23 us (3%)
    all_to_all x4, waiting for transfers between devices, swap_devices(): return lax.all_to_all(blocks, BOTH, split_axis=0, concat_axis=0, tiled=True)  72.3 us
    pallas_call x2, Pallas kernels, mid(): pl.pallas_call(functools.partial(mid_kernel, packed), grid=(samples,), in...  70.5 us
    all_to_all x4, starting transfers between devices, swap_devices(): return lax.all_to_all(blocks, BOTH, split_axis=0, concat_axis=0, tiled=True)  33.9 us
    pallas_call x2, Pallas kernels, pre(): pl.pallas_call(kernel, grid=(rows // 2,), in_specs=[pl.BlockSpec((2, lon_...  23.7 us
    pallas_call x2, Pallas kernels, post(): pl.pallas_call(functools.partial(post_kernel, packed), in_specs=[ANY, ANY...  20.9 us
    another operation x4, other arithmetic, filter_chunk(): return jnp.stack([lay(real, real), lay(-imag, imag)])  5.4 us
  transfers between devices with their start and end apart: 4, of which 4 were waited for; matrix products, arithmetic and copies ran while one was open for 7% of the time, Pallas kernels for 39%

profile of v4, /device:TPU:14, one launch (start us, length us, event | category | flops | bytes accessed | tf_op | source)
XLA Modules:
  0.0 239.9 jit_solution(2766789878988093515)
XLA Ops:
  0.0 10.9 %row_forward.3 = bf16[64,2,5,8,384]{4,3,2,1,0:T(8,128)(2,1)} custom-call(bf16[10,720,512]{2,1,0:T(8,128)(2,1)} %bitcast.18, f32[1,512]{1,0:T(1,128)} %bitcast.28, f32[1,512]{1,0:T(1,128)} %bitcast.30, bf16[384,720]{1,0:T(8,128)(2,1)} %constant.21.clone.table_ref), custom_call_target="tpu_custom_call" | custom-call | flops 2831155200 | bytes 11304960 | tf_op jit(solution)/shard_map/row_forward/pallas_call | solution.py:168
  10.9 10.8 %all-to-all-start.2 = ((bf16[128,5,8,384]{3,2,1,0:T(8,128)(2,1)}), bf16[128,5,8,384]{3,2,1,0:T(8,128)(2,1)}, u32[]{:S(2)}, u32[]{:S(2)}) async-start(bf16[128,5,8,384]{3,2,1,0:T(8,128)(2,1)} %bitcast.25), calls=%async_computation.2 | async-start | bytes 7864320 | tf_op jit(solution)/shard_map/all_to_all | solution.py:398
  21.7 2.9 %copy.13 = f32[4,320,722]{2,1,0:T(8,128)S(1)} copy(f32[4,320,722]{2,0,1:T(4,128)} %bitcast.27) | data formatting | bytes 7393280 | tf_op jit(solution)/shard_map/transpose | solution.py:380
  24.6 1.8 fusion.3
  26.9 0.7 fusion.2
  27.7 0.9 slice.81
  28.6 0.9 pad_slice_fusion
  29.5 0.9 fusion
  30.4 12.8 %row_forward.2 = bf16[64,2,14,8,128]{4,3,2,1,0:T(8,128)(2,1)} custom-call(bf16[10,720,512]{2,1,0:T(8,128)(2,1)} %bitcast.19, f32[1,512]{1,0:T(1,128)} %bitcast.29, f32[1,512]{1,0:T(1,128)} %bitcast.31, bf16[384,720]{1,0:T(8,128)(2,1)} %constant.22.clone.table_ref, bf16[768,720]{1,0:T(8,128)(2,1)} %constant.23.clone.last_ref), custom_call_target="tpu_custom_call" | custom-call | flops 2831155200 | bytes 11304960 | tf_op jit(solution)/shard_map/row_forward/pallas_call | solution.py:168
  43.3 1.9 fusion.4
  46.5 0.7 copy-done.2
  48.0 2.2 pad_maximum_fusion.filt_ref
  50.7 2.2 pad_maximum_fusion.1.filt_ref
  52.9 16.2 %all-to-all-done.2.x_ref = bf16[128,5,8,384]{3,2,1,0:T(8,128)(2,1)} async-done(((bf16[128,5,8,384]{3,2,1,0:T(8,128)(2,1)}), bf16[128,5,8,384]{3,2,1,0:T(8,128)(2,1)}, u32[]{:S(2)}, u32[]{:S(2)}) %all-to-all-start.2) | async-done | bytes 3932192 | tf_op jit(solution)/shard_map/all_to_all | solution.py:398
  69.1 7.8 %all-to-all-start = ((bf16[128,14,8,128]{3,2,1,0:T(8,128)(2,1)}), bf16[128,14,8,128]{3,2,1,0:T(8,128)(2,1)}, u32[]{:S(2)}, u32[]{:S(2)}) async-start(bf16[128,14,8,128]{3,2,1,0:T(8,128)(2,1)} %bitcast.26), calls=%async_computation | async-start | bytes 7340032 | tf_op jit(solution)/shard_map/all_to_all | solution.py:398
  76.9 35.1 %columns.3 = bf16[128,5,8,384]{3,2,1,0:T(8,128)(2,1)} custom-call(bf16[128,5,8,384]{3,2,1,0:T(8,128)(2,1)} %all-to-all-done.2.x_ref, f32[2,1280,384]{2,1,0:T(8,128)} %pad_maximum_fusion.filt_ref, bf16[1280,2560]{1,0:T(8,128)(2,1)} %constant.19.clone.forward_ref, bf16[1280,2560]{1,0:T(8,128)(2,1)} %constant.20.clone.inverse_ref), custom_call_target="tpu_custom_call" | custom-call | flops 20132659200 | bytes 24903680 | tf_op jit(solution)/shard_map/columns/pallas_call | solution.py:264
  112.0 9.4 %all-to-all-done.x_ref = bf16[128,14,8,128]{3,2,1,0:T(8,128)(2,1)} async-done(((bf16[128,14,8,128]{3,2,1,0:T(8,128)(2,1)}), bf16[128,14,8,128]{3,2,1,0:T(8,128)(2,1)}, u32[]{:S(2)}, u32[]{:S(2)}) %all-to-all-start) | async-done | bytes 3670048 | tf_op jit(solution)/shard_map/all_to_all | solution.py:398
  121.4 7.6 %all-to-all-start.3 = ((bf16[128,5,8,384]{3,2,1,0:T(8,128)(2,1)}), bf16[128,5,8,384]{3,2,1,0:T(8,128)(2,1)}, u32[]{:S(2)}, u32[]{:S(2)}) async-start(bf16[128,5,8,384]{3,2,1,0:T(8,128)(2,1)} %columns.3), calls=%async_computation.3 | async-start | bytes 7864320 | tf_op jit(solution)/shard_map/all_to_all | solution.py:398
  129.0 35.4 %columns.2 = bf16[128,14,8,128]{3,2,1,0:T(8,128)(2,1)} custom-call(bf16[128,14,8,128]{3,2,1,0:T(8,128)(2,1)} %all-to-all-done.x_ref, f32[2,1280,384]{2,1,0:T(8,128)} %pad_maximum_fusion.1.filt_ref, bf16[1280,2560]{1,0:T(8,128)(2,1)} %constant.19.clone.forward_ref, bf16[1280,2560]{1,0:T(8,128)(2,1)} %constant.20.clone.inverse_ref), custom_call_target="tpu_custom_call" | custom-call | flops 20132659200 | bytes 24903680 | tf_op jit(solution)/shard_map/columns/pallas_call | solution.py:264
  164.5 12.0 %all-to-all-done.3 = bf16[128,5,8,384]{3,2,1,0:T(8,128)(2,1)} async-done(((bf16[128,5,8,384]{3,2,1,0:T(8,128)(2,1)}), bf16[128,5,8,384]{3,2,1,0:T(8,128)(2,1)}, u32[]{:S(2)}, u32[]{:S(2)}) %all-to-all-start.3) | async-done | bytes 3932192 | tf_op jit(solution)/shard_map/all_to_all | solution.py:398
  176.5 7.8 %all-to-all-start.1 = ((bf16[128,14,8,128]{3,2,1,0:T(8,128)(2,1)}), bf16[128,14,8,128]{3,2,1,0:T(8,128)(2,1)}, u32[]{:S(2)}, u32[]{:S(2)}) async-start(bf16[128,14,8,128]{3,2,1,0:T(8,128)(2,1)} %columns.2), calls=%async_computation.1 | async-start | bytes 7340032 | tf_op jit(solution)/shard_map/all_to_all | solution.py:398
  184.3 9.9 %row_inverse.2.x_hbm = bf16[10,720,512]{2,1,0:T(8,128)(2,1)} custom-call(bf16[64,2,5,8,384]{4,3,2,1,0:T(8,128)(2,1)} %bitcast.12.back_hbm, bf16[10,720,512]{2,1,0:T(8,128)(2,1)} %bitcast.20, bf16[720,384]{1,0:T(8,128)(2,1)} %constant.24.clone.refs_0_), custom_call_target="tpu_custom_call" | custom-call | flops 2831155200 | bytes 18677760 | tf_op jit(solution)/shard_map/row_inverse/pallas_call | solution.py:358
  194.2 34.6 %all-to-all-done.1 = bf16[128,14,8,128]{3,2,1,0:T(8,128)(2,1)} async-done(((bf16[128,14,8,128]{3,2,1,0:T(8,128)(2,1)}), bf16[128,14,8,128]{3,2,1,0:T(8,128)(2,1)}, u32[]{:S(2)}, u32[]{:S(2)}) %all-to-all-start.1) | async-done | bytes 3670048 | tf_op jit(solution)/shard_map/all_to_all | solution.py:398
  228.8 11.0 %row_inverse.3 = bf16[10,720,512]{2,1,0:T(8,128)(2,1)} custom-call(bf16[64,2,14,8,128]{4,3,2,1,0:T(8,128)(2,1)} %bitcast.10.back_hbm, bf16[10,720,512]{2,1,0:T(8,128)(2,1)} %row_inverse.2.x_hbm, bf16[720,384]{1,0:T(8,128)(2,1)} %constant.25.clone.refs_0_, bf16[720,768]{1,0:T(8,128)(2,1)} %constant.26.clone.refs_1_), custom_call_target="tpu_custom_call" | custom-call | flops 2831155200 | bytes 18677760 | tf_op jit(solution)/shard_map/row_inverse/pallas_call | solution.py:358
  (16 shorter events, 3.1 us)
Async XLA Ops:
  10.9 58.2 %all-to-all-start.2 = ((bf16[128,5,8,384]{3,2,1,0:T(8,128)(2,1)}), bf16[128,5,8,384]{3,2,1,0:T(8,128)(2,1)}, u32[]{:S(2)}, u32[]{:S(2)}) async-start(bf16[128,5,8,384]{3,2,1,0:T(8,128)(2,1)} %bitcast.25), calls=%async_computation.2 | async-start | bytes 7864320 | tf_op jit(solution)/shard_map/all_to_all | solution.py:398
  24.6 2.4 copy-start
  43.2 2.7 %copy-start.1 = (f32[4,320,722]{2,1,0:T(8,128)S(1)}, f32[4,320,722]{2,1,0:T(8,128)}, u32[]{:S(2)}) copy-start(f32[4,320,722]{2,1,0:T(8,128)} %copy-done) | copy-start | bytes 11089924
  46.0 1.3 copy-start.2
  46.0 1.5 copy-start.3
  48.0 2.2 copy-start.4
  48.0 2.2 copy-start.5
  69.1 52.3 %all-to-all-start = ((bf16[128,14,8,128]{3,2,1,0:T(8,128)(2,1)}), bf16[128,14,8,128]{3,2,1,0:T(8,128)(2,1)}, u32[]{:S(2)}, u32[]{:S(2)}) async-start(bf16[128,14,8,128]{3,2,1,0:T(8,128)(2,1)} %bitcast.26), calls=%async_computation | async-start | bytes 7340032 | tf_op jit(solution)/shard_map/all_to_all | solution.py:398
  121.4 55.0 %all-to-all-start.3 = ((bf16[128,5,8,384]{3,2,1,0:T(8,128)(2,1)}), bf16[128,5,8,384]{3,2,1,0:T(8,128)(2,1)}, u32[]{:S(2)}, u32[]{:S(2)}) async-start(bf16[128,5,8,384]{3,2,1,0:T(8,128)(2,1)} %columns.3), calls=%async_computation.3 | async-start | bytes 7864320 | tf_op jit(solution)/shard_map/all_to_all | solution.py:398
  176.5 52.3 %all-to-all-start.1 = ((bf16[128,14,8,128]{3,2,1,0:T(8,128)(2,1)}), bf16[128,14,8,128]{3,2,1,0:T(8,128)(2,1)}, u32[]{:S(2)}, u32[]{:S(2)}) async-start(bf16[128,14,8,128]{3,2,1,0:T(8,128)(2,1)} %columns.2), calls=%async_computation.1 | async-start | bytes 7340032 | tf_op jit(solution)/shard_map/all_to_all | solution.py:398
